TPU v7x, 32 devices: a whole 2x2x4 slice. The times are simulated.
32 devices in a mesh: dp: 8 (over z, y), feat: 4 (over x, core).
Axes of the slice: x: 2, y: 2, z: 4, core: 2. Of those that a mesh axis runs over, the one named last changes fastest.
Arguments:
- activations: bfloat16 [8192, 8192], P('dp', 'feat'), may hold values from -6 to 6
- cand_index: int32 [8192], P('dp'), may hold values from 0 to 7
- labels: int32 [512], P('dp'), may hold values 0 or 1
- counts: int32 [8], P('dp'), may hold values from 1 to 64, as said below
Outputs:
- scores: float32 [8192, 8], P('dp', 'feat')
Inputs may be any that keep to these rules, and one draw needn't show every extreme that they name: `counts`: the fullest slab has all 64 prompt slots live.
All inputs are finite; a program needn't handle non-finite values. No bound on the sum of `labels` on one device may be relied on, other than what follows from the above.
Results may differ from a plain program's by a relative error of at most 0.0047.
Values may be sent and summed in bfloat16 or wider, within the bound.
No kernel may reach another device: no remote copies, remote signals or barrier semaphores. Data moves between devices by JAX's collectives and lax.ppermute only.
A program may use at most 64 MiB of HBM per device.

v0:
```python
import jax
import jax.numpy as jnp
from jax import lax
from jax.sharding import PartitionSpec as P

CAND_DEV = 1
PER_PROMPT = 16


epsilon = 1e-06


def project(activations, dir_block):
    return lax.dot_general(
        activations, dir_block, (((1,), (1,)), ((), ())), preferred_element_type=jnp.float32
    )


def per_device(activations, cand_index, labels, counts):
    row_total = activations.shape[0]
    cand_total = CAND_DEV * lax.axis_size("dp")
    prompt_of = jnp.arange(row_total, dtype=jnp.int32) // PER_PROMPT
    live = prompt_of < counts[0]
    classes = jnp.repeat(labels, PER_PROMPT)
    cand_ids = jnp.arange(cand_total, dtype=jnp.int32)
    matches = (cand_index[None, :] == cand_ids[:, None]) & live[None, :]
    harmful_hits = matches & (classes[None, :] == 1)
    harmless_hits = matches & (classes[None, :] == 0)
    member = jnp.concatenate([harmful_hits, harmless_hits], axis=0).astype(jnp.bfloat16)
    class_sums = jnp.dot(member, activations, preferred_element_type=jnp.float32).reshape(
        2, cand_total, -1
    )
    class_counts = jnp.sum(member.astype(jnp.float32), axis=1).reshape(2, cand_total)
    owned_sums, owned_counts = (
        lax.psum_scatter(class_sums, "dp", scatter_dimension=1, tiled=True),
        lax.psum_scatter(class_counts, "dp", scatter_dimension=1, tiled=True),
    )
    harmful_mean = owned_sums[0] / jnp.maximum(owned_counts[0], 1.0)[:, None]
    harmless_mean = owned_sums[1] / jnp.maximum(owned_counts[1], 1.0)[:, None]
    raw_float = harmful_mean - harmless_mean
    raw_dir = raw_float.astype(jnp.bfloat16)
    squares = jnp.sum(jnp.square(raw_dir.astype(jnp.float32)), axis=1)
    total_sq = lax.psum(squares, "feat")
    inv_norm = lax.rsqrt(total_sq + epsilon).astype(jnp.bfloat16)
    dir_block = lax.all_gather(raw_dir, "dp", axis=0, tiled=True)
    inv_block = lax.all_gather(inv_norm, "dp", axis=0, tiled=True)
    partial_value = project(activations, dir_block) * inv_block.astype(jnp.float32)[None, :]
    return lax.psum_scatter(partial_value, "feat", scatter_dimension=1, tiled=True)


def solution(mesh):
    return jax.shard_map(
        per_device,
        mesh=mesh,
        in_specs=(P("dp", "feat"), P("dp"), P("dp"), P("dp")),
        out_specs=P("dp", "feat"),
        check_vma=False,
    )
```

profile of v0, /device:TPU:0, one launch (start us, length us, event | category | flops | bytes accessed | tf_op | source)
XLA Modules:
  0.0 168.1 jit_solution(5908991138944723155)
XLA Ops:
  6.5 0.7 broadcast_compare_fusion.1
  7.2 0.1 broadcast_in_dim.4
  7.3 0.1 eq.43
  7.4 0.1 broadcast_in_dim.5
  7.5 0.1 eq.45
  8.2 0.7 fusion.5
  9.0 2.8 %convolution_bitcast_fusion = f32[2,8,2048]{2,1,0:T(8,128)S(1)} fusion(bf16[1024,2048]{1,0:T(8,128)(2,1)} %param.4, pred[8,1024]{1,0:T(8,128)(4,1)S(1)} %get-tuple-element.8, pred[8,1024]{1,0:T(8,128)(4,1)S(1)} %get-tuple-element.7), kind=kOutput, calls=%fused_computation | convolution fusion | flops 67125248 | bytes 4341760 | tf_op jit(solution)/shard_map/dot_general | solution.py:30
  11.8 0.8 copy.8
  12.6 0.1 convert_reduce_fusion
  12.7 0.1 reshape.108
  12.8 23.1 %all-reduce.2 = f32[2,8]{1,0:T(2,128)S(1)} all-reduce(f32[2,8]{1,0:T(2,128)S(1)} %reshape.108), channel_id=4, replica_groups=mesh['dp'=8,'feat'=4] {'dp'}, use_global_device_ids=true, to_apply=%region_2.3.clone | all-reduce | flops 16 | bytes 128
  35.9 0.6 fusion.12
  36.5 0.7 constant_dynamic-slice_fusion.1
  37.2 0.6 fusion.11
  39.1 0.6 dynamic-slice.5
  39.8 45.3 %all-reduce.6.cloned.1.call-done = f32[2,8,2048]{2,0,1:T(2,128)} async-done(((f32[2,8,2048]{2,0,1:T(2,128)}), f32[2,8,2048]{2,0,1:T(2,128)}) %all-reduce.6.cloned.1.call-update) | async-done | bytes 131088
  85.1 2.0 %multiply_reduce_fusion = (f32[]{:T(128)}, bf16[1,1,2048]{2,0,1:T(2,128)(2,1)S(1)}) fusion(f32[]{:T(128)} %bitcast.3, f32[2,8,2048]{2,0,1:T(2,128)} %all-reduce.6.cloned.1.call-done, u32[]{:T(128)S(6)} %convert, u32[]{:T(128)} %bitcast.10, f32[]{:T(128)} %bitcast.2), kind=kLoop, calls=%fused_computation.12 | loop fusion | flops 14335 | bytes 20500 | tf_op jit(solution)/shard_map/reduce_sum | solution.py:42
  87.1 6.3 %psum.7 = f32[1]{0:T(128)} all-reduce(f32[1]{0:T(128)} %bitcast.5), channel_id=1, replica_groups=mesh['dp'=8,'feat'=4] {'feat'}, use_global_device_ids=true, to_apply=%region_4.5 | all-reduce | flops 1 | bytes 8 | tf_op jit(solution)/shard_map/psum | solution.py:43
  94.7 1.4 dynamic-update-slice
  96.7 19.7 %all-reduce = bf16[8]{0:T(256)(128)(2,1)S(1)} all-reduce(bf16[8]{0:T(256)(128)(2,1)S(1)} %dynamic-update-slice), channel_id=1, replica_groups=mesh['dp'=8,'feat'=4] {'dp'}, use_global_device_ids=true, to_apply=%add | all-reduce | flops 8 | bytes 32
  116.5 30.5 %all-gather = bf16[8,1,2048]{2,1,0:T(2,128)(2,1)S(1)} all-gather(bf16[1,1,2048]{2,1,0:T(2,128)(2,1)S(1)} %bitcast.22), channel_id=2, replica_groups=mesh['dp'=8,'feat'=4] {'dp'}, dimensions={0}, use_global_device_ids=true | all-gather | bytes 36864 | tf_op jit(solution)/shard_map/all_gather | solution.py:45
  147.0 3.4 %fusion = f32[1024,8]{0,1:T(8,128)S(1)} fusion(bf16[1024,2048]{1,0:T(8,128)(2,1)} %param.4, bf16[8,1,2048]{2,1,0:T(2,128)(2,1)S(1)} %all-gather, f32[8]{0:T(128)S(1)} %convert_element_type.47), kind=kOutput, calls=%fused_computation.2 | convolution fusion | flops 33562624 | bytes 4259872 | tf_op jit(solution)/shard_map/dot_general | solution.py:14
  150.3 10.3 %all-reduce.3 = f32[1024,8]{0,1:T(8,128)S(1)} all-reduce(f32[1024,8]{0,1:T(8,128)S(1)} %fusion), channel_id=5, replica_groups=mesh['dp'=8,'feat'=4] {'feat'}, use_global_device_ids=true, to_apply=%region_5.6.clone | all-reduce | flops 8192 | bytes 65536
  160.6 0.6 constant_dynamic-slice_fusion
  (9 shorter events, 0.0 us)
Async XLA Ops:
  6.5 29.4 %copy-start = (u32[32]{0:T(128)S(1)}, u32[32]{0:T(128)}, u32[]{:S(2)}) copy-start(u32[32]{0:T(128)} %constant.31) | copy-start | bytes 388
  6.5 32.6 %copy-start.1 = (u32[32]{0:T(128)S(1)}, u32[32]{0:T(128)}, u32[]{:S(2)}) copy-start(u32[32]{0:T(128)} %constant.45) | copy-start | bytes 388
  6.5 78.5 %all-reduce.6.cloned.1.call-start = ((), (), s32[]{:S(2)}) async-start(), calls=%async_computation | async-start | bytes 262144
Sparse Core Ops, SparseCore 0:
  12.7 72.3 all-reduce.5
where the time goes:
time: 169 us; the launch traced here: 168 us
  blocking collectives  89.9 us (53%)
  waiting for transfers between devices  45.3 us (27%)
  between operations  17.3 us (10%)
  matrix products  6.21 us (4%)
  local copies, waits for them, and re-layouts  5.75 us (3%)
  other arithmetic  3.58 us (2%)
    unnamed x3, blocking collectives  53.1 us
    unnamed x2, waiting for transfers between devices  45.3 us
    all_gather x1, blocking collectives, per_device(): dir_block = lax.all_gather(raw_dir, 'dp', axis=0, tiled=True)  30.5 us
    psum x1, blocking collectives, per_device(): total_sq = lax.psum(squares, 'feat')  6.33 us
    unnamed x10, local copies, waits for them, and re-layouts  3.97 us
  transfers between devices with their start and end apart: 1, of which 1 were waited for; matrix products, arithmetic and copies ran while one was open for 2% of the time, Pallas kernels for 0%

commit v1 on v0

v1 whole, which is shorter than its diff:
```python
import functools

import jax
import jax.numpy as jnp
from jax import lax
from jax.experimental import pallas as pl
from jax.experimental.pallas import tpu as pltpu
from jax.sharding import PartitionSpec as P

CAND_DEV = 1
PER_PROMPT = 16
LANES = 128
VMEM_LIMIT = 32 * 1024 * 1024

epsilon = 1e-06


def sums_kernel(steps, counts_ref, cand_ref, labels_ref, acts_hbm, sums_ref, acts_ref, sems):
    rows, width = acts_ref.shape
    classes = sums_ref.shape[0]
    cands = classes // 2
    prompts = labels_ref.shape[1]
    tall = rows // steps

    def fetch(step):
        part = pl.ds(step * tall, tall)
        return pltpu.make_async_copy(acts_hbm.at[part, :], acts_ref.at[part, :], sems.at[step])

    for step in range(steps):
        fetch(step).start()

    prompt_ids = lax.broadcasted_iota(jnp.int32, (prompts, rows), 0)
    prompt_of = lax.broadcasted_iota(jnp.int32, (prompts, rows), 1) // PER_PROMPT
    spread = jnp.where(prompt_ids == prompt_of, 1.0, 0.0).astype(jnp.bfloat16)
    labels = jnp.broadcast_to(labels_ref[...].astype(jnp.float32), (8, prompts))
    row_class = jnp.dot(labels.astype(jnp.bfloat16), spread, preferred_element_type=jnp.float32)[:1]
    live = lax.broadcasted_iota(jnp.int32, (1, rows), 1) // PER_PROMPT < counts_ref[0]
    wanted = lax.broadcasted_iota(jnp.int32, (classes, rows), 0)
    slot = jnp.where(row_class == 1.0, cand_ref[...], cand_ref[...] + cands)
    slot = jnp.where(live, slot, -1)
    member_float = jnp.where(wanted == slot, 1.0, 0.0)
    member = member_float.astype(jnp.bfloat16)
    tally = jnp.sum(member_float, axis=1, keepdims=True)
    sums_ref[:, width:] = jnp.broadcast_to(tally, (classes, LANES))

    total = None
    for step in range(steps):
        fetch(step).wait()
        piece = jnp.dot(
            member[:, step * tall : (step + 1) * tall],
            acts_ref[step * tall : (step + 1) * tall, :],
            preferred_element_type=jnp.float32,
        )
        total = piece if total is None else total + piece
    sums_ref[:, :width] = total


def class_sums(activations, cand_index, labels, counts, classes, steps=8):
    rows, width = activations.shape
    vmem = pl.BlockSpec(memory_space=pltpu.VMEM)
    return pl.pallas_call(
        functools.partial(sums_kernel, steps),
        out_shape=(
            jax.ShapeDtypeStruct((classes, width + LANES), jnp.float32),
            pltpu.VMEM((rows, width), activations.dtype),
        ),
        in_specs=[
            pl.BlockSpec(memory_space=pltpu.SMEM),
            vmem,
            vmem,
            pl.BlockSpec(memory_space=pltpu.HBM),
        ],
        out_specs=(vmem, vmem),
        scratch_shapes=[pltpu.SemaphoreType.DMA((steps,))],
        compiler_params=pltpu.CompilerParams(vmem_limit_bytes=VMEM_LIMIT),
        name="class_sums",
    )(counts, cand_index.reshape(1, rows), labels.reshape(1, -1), pltpu.with_memory_space_constraint(activations, pltpu.HBM))


def project_kernel(upper_ref, mine_ref, other_ref, acts_ref, keep_ref, send_ref):
    rows, width = acts_ref.shape
    cands = mine_ref.shape[0] // 2
    half = cands // 2
    total = mine_ref[...] + other_ref[...]
    tally = jnp.maximum(total[:, width : width + 1], 1.0)
    harmful_mean = total[:cands, :width] / tally[:cands]
    harmless_mean = total[cands:, :width] / tally[cands:]
    raw_dir = (harmful_mean - harmless_mean).astype(jnp.bfloat16)
    squares = jnp.sum(jnp.square(raw_dir.astype(jnp.float32)), axis=1, keepdims=True)
    squares = jnp.broadcast_to(squares, (cands, LANES))
    plain = lax.dot_general(
        raw_dir, acts_ref[...], (((1,), (1,)), ((), ())), preferred_element_type=jnp.float32
    )
    upper = upper_ref[0] == 1
    keep_ref[:, :rows] = jnp.where(upper, plain[half:], plain[:half])
    send_ref[:, :rows] = jnp.where(upper, plain[:half], plain[half:])
    keep_ref[:, rows:] = jnp.where(upper, squares[half:], squares[:half])
    send_ref[:, rows:] = jnp.where(upper, squares[:half], squares[half:])


def project(upper, mine, other, acts):
    rows = acts.shape[0]
    cands = mine.shape[0] // 2
    vmem = pl.BlockSpec(memory_space=pltpu.VMEM)
    half = jax.ShapeDtypeStruct((cands // 2, rows + LANES), jnp.float32)
    return pl.pallas_call(
        project_kernel,
        out_shape=(half, half),
        in_specs=[pl.BlockSpec(memory_space=pltpu.SMEM), vmem, vmem, vmem],
        out_specs=(vmem, vmem),
        compiler_params=pltpu.CompilerParams(vmem_limit_bytes=VMEM_LIMIT),
        name="project",
    )(upper, mine, other, pltpu.with_memory_space_constraint(acts, pltpu.VMEM))


def trade(value, axis, bit):
    return lax.ppermute(value, axis, [(i, i ^ bit) for i in range(lax.axis_size(axis))])


def per_device(activations, cand_index, labels, counts):
    rows = activations.shape[0]
    dp, feat = lax.axis_size("dp"), lax.axis_size("feat")
    cands = CAND_DEV * dp
    sums, acts = class_sums(activations, cand_index, labels, counts, 2 * cands)

    bit = 1
    while 2 * bit < dp:
        sums = sums + trade(sums, "dp", bit)
        bit *= 2
    other = trade(sums, "dp", bit)

    place = lax.axis_index("feat")
    bit = feat // 2
    upper = (place // bit % 2).astype(jnp.int32).reshape(1)
    keep, send = project(upper, sums, other, acts)
    keep = keep + trade(send, "feat", bit)
    while bit > 1:
        bit //= 2
        half = keep.shape[0] // 2
        upper = place // bit % 2 == 1
        low, high = keep[:half], keep[half:]
        keep = jnp.where(upper, high, low) + trade(jnp.where(upper, low, high), "feat", bit)
    inv_norm = lax.rsqrt(keep[:, rows : rows + 1] + epsilon).astype(jnp.bfloat16)
    return (keep[:, :rows] * inv_norm.astype(jnp.float32)).T


def solution(mesh):
    return jax.shard_map(
        per_device,
        mesh=mesh,
        in_specs=(P("dp", "feat"), P("dp"), P("dp"), P("dp")),
        out_specs=P("dp", "feat"),
        check_vma=False,
    )
```

time: 169 us -> 35.2 us (0.21)
  blocking collectives: 89.9 us -> 0 us
  waiting for transfers between devices: 45.3 us -> 15.1 us
  between operations: 17.3 us -> 0.7 us
  starting transfers between devices: 0.01 us -> 9.37 us
  matrix products: 6.21 us -> 0 us
  Pallas kernels: 0 us -> 3.6 us
  other arithmetic: 3.58 us -> 0.86 us
    unnamed x3 -> x0, blocking collectives: 53.1 us -> none
    unnamed x2 -> x0, waiting for transfers between devices: 45.3 us -> none
    all_gather x1 -> x0, blocking collectives: 30.5 us -> none  [per_device(): dir_block = lax.all_gather(raw_dir, 'dp', axis=0, tiled=True)]
    ppermute x0 -> x5, waiting for transfers between devices: none -> 15.1 us  [trade(): lax.ppermute(value, axis, [(i, i ^ bit) for i in range(lax.axis_size(axis...]
    ppermute x0 -> x5, starting transfers between devices: none -> 9.37 us  [trade(): lax.ppermute(value, axis, [(i, i ^ bit) for i in range(lax.axis_size(axis...]
    psum x1 -> x0, blocking collectives: 6.33 us -> none  [per_device(): total_sq = lax.psum(squares, 'feat')]
    dot_general x2 -> x0, matrix products: 6.21 us -> none  [the longest x1 3.37 us: project(): lax.dot_general(activations, dir_block, (((1,), (1,)), ((), ())), preferr...]
    pallas_call x0 -> x2, Pallas kernels: none -> 3.6 us  [the longest x1 2.4 us: class_sums(): pl.pallas_call(functools.partial(sums_kernel, steps), out_shape=(jax.Shap...]
  transfers between devices with their start and end apart: 1 -> 5, of which waited for: 1 -> 5; matrix products, arithmetic and copies ran while one was open for 2% -> 0% of each run, Pallas kernels for 0% -> 0%
where the time goes in v1:
time: 35.2 us; the launch traced here: 35 us
  waiting for transfers between devices  15.1 us (43%)
  starting transfers between devices  9.37 us (27%)
  local copies, waits for them, and re-layouts  5.45 us (15%)
  Pallas kernels  3.6 us (10%)
  other arithmetic  0.86 us (2%)
  between operations  0.7 us (2%)
    ppermute x5, waiting for transfers between devices, trade(): lax.ppermute(value, axis, [(i, i ^ bit) for i in range(lax.axis_size(axis...  15.1 us
    ppermute x5, starting transfers between devices, trade(): lax.ppermute(value, axis, [(i, i ^ bit) for i in range(lax.axis_size(axis...  9.37 us
    unnamed x8, local copies, waits for them, and re-layouts  5.45 us
    pallas_call x1, Pallas kernels, class_sums(): pl.pallas_call(functools.partial(sums_kernel, steps), out_shape=(jax.Shap...  2.4 us
    pallas_call x1, Pallas kernels, project(): pl.pallas_call(project_kernel, out_shape=(half, half), in_specs=[pl.Block...  1.2 us
  transfers between devices with their start and end apart: 5, of which 5 were waited for; matrix products, arithmetic and copies ran while one was open for 0% of the time, Pallas kernels for 0%

profile of v1, /device:TPU:0, one launch (start us, length us, event | category | flops | bytes accessed | tf_op | source)
XLA Modules:
  0.0 35.0 jit_solution(13114477171311800892)
XLA Ops:
  0.7 0.0 copy-start.2
  0.7 0.7 %copy-done.2 = s32[1024]{0:T(1024)S(1)} copy-done((s32[1024]{0:T(1024)S(1)}, s32[1024]{0:T(1024)}, u32[]{:S(2)}) %copy-start.2) | copy-done | bytes 4120
  1.3 0.0 copy-start.3
  1.3 0.7 %copy-done.3 = s32[64]{0:T(128)S(1)} copy-done((s32[64]{0:T(128)S(1)}, s32[64]{0:T(128)}, u32[]{:S(2)}) %copy-start.3) | copy-done | bytes 280
  2.0 2.4 %class_sums.1 = (f32[16,2176]{1,0:T(8,128)S(1)}, bf16[1024,2048]{1,0:T(8,128)(2,1)S(1)}) custom-call(s32[1]{0:T(128)S(6)} %copy.5.counts_ref, s32[1,1024]{1,0:T(1,128)S(1)} %bitcast.5, s32[1,64]{1,0:T(1,128)S(1)} %bitcast.6, bf16[1024,2048]{1,0:T(8,128)(2,1)} %acts_hbm.1), custom_call_target="tpu_custom_call" | custom-call | tf_op jit(solution)/shard_map/class_sums/pallas_call | solution.py:61
  4.4 0.0 copy-start
  4.4 1.9 %copy-done = bf16[1024,2048]{1,0:T(8,128)(2,1)} copy-done((bf16[1024,2048]{1,0:T(8,128)(2,1)}, bf16[1024,2048]{1,0:T(8,128)(2,1)S(1)}, u32[]{:S(2)}) %copy-start) | copy-done | bytes 4194328
  6.3 3.0 %collective-permute-start = (f32[16,2176]{1,0:T(8,128)S(1)}, f32[16,2176]{1,0:T(8,128)S(1)}, u32[]{:S(2)}, u32[]{:S(2)}) collective-permute-start(f32[16,2176]{1,0:T(8,128)S(1)} %get-tuple-element.9), channel_id=1, source_target_pairs={{0,4},{4,0},{8,12},{12,8},{16,20},{20,16},{24,28},{28,24},{1,5},{5... | collective-permute-start | bytes 417800 | tf_op jit(solution)/shard_map/ppermute | solution.py:117
  9.3 3.7 %collective-permute-done = f32[16,2176]{1,0:T(8,128)S(1)} collective-permute-done((f32[16,2176]{1,0:T(8,128)S(1)}, f32[16,2176]{1,0:T(8,128)S(1)}, u32[]{:S(2)}, u32[]{:S(2)}) %collective-permute-start) | collective-permute-done | bytes 139296 | tf_op jit(solution)/shard_map/ppermute | solution.py:117
  13.0 1.9 %collective-permute-start.1 = (f32[16,2176]{1,0:T(8,128)S(1)}, f32[16,2176]{1,0:T(8,128)S(1)}, u32[]{:S(2)}, u32[]{:S(2)}) collective-permute-start(f32[16,2176]{1,0:T(8,128)S(1)} %add.26), channel_id=1, source_target_pairs={{0,8},{4,12},{8,0},{12,4},{16,24},{20,28},{24,16},{28,20},{1,9},{5... | collective-permute-start | bytes 417800 | tf_op jit(solution)/shard_map/ppermute | solution.py:117
  14.9 3.3 %collective-permute-done.1 = f32[16,2176]{1,0:T(8,128)S(1)} collective-permute-done((f32[16,2176]{1,0:T(8,128)S(1)}, f32[16,2176]{1,0:T(8,128)S(1)}, u32[]{:S(2)}, u32[]{:S(2)}) %collective-permute-start.1) | collective-permute-done | bytes 139296 | tf_op jit(solution)/shard_map/ppermute | solution.py:117
  18.1 2.9 %collective-permute-start.2 = (f32[16,2176]{1,0:T(8,128)S(1)}, f32[16,2176]{1,0:T(8,128)S(1)}, u32[]{:S(2)}, u32[]{:S(2)}) collective-permute-start(f32[16,2176]{1,0:T(8,128)S(1)} %add.27.mine_ref), channel_id=1, source_target_pairs={{0,16},{4,20},{8,24},{12,28},{16,0},{20,4},{24,8},{28,12},{1,17},{... | collective-permute-start | bytes 417800 | tf_op jit(solution)/shard_map/ppermute | solution.py:117
  21.0 4.8 %collective-permute-done.2.other_ref = f32[16,2176]{1,0:T(8,128)S(1)} collective-permute-done((f32[16,2176]{1,0:T(8,128)S(1)}, f32[16,2176]{1,0:T(8,128)S(1)}, u32[]{:S(2)}, u32[]{:S(2)}) %collective-permute-start.2) | collective-permute-done | bytes 139296 | tf_op jit(solution)/shard_map/ppermute | solution.py:117
  25.8 0.0 copy-start.1
  25.8 2.2 %copy-done.1 = bf16[1024,2048]{1,0:T(8,128)(2,1)S(1)} copy-done((bf16[1024,2048]{1,0:T(8,128)(2,1)S(1)}, bf16[1024,2048]{1,0:T(8,128)(2,1)}, u32[]{:S(2)}) %copy-start.1) | copy-done | bytes 4194328
  28.0 1.2 %project.1 = (f32[4,1152]{1,0:T(4,128)S(1)}, f32[4,1152]{1,0:T(4,128)S(1)}) custom-call(s32[1]{0:T(128)} %bitcast.upper_ref, f32[16,2176]{1,0:T(8,128)S(1)} %add.27.mine_ref, f32[16,2176]{1,0:T(8,128)S(1)} %collective-permute-done.2.other_ref, bf16[1024,2048]{1,0:T(8,128)(2,1)S(1)} %copy-done.1), custom_call_target="tpu_custom_call" | custom-call | tf_op jit(solution)/shard_map/project/pallas_call | solution.py:106
  29.2 1.6 %collective-permute-start.3 = (f32[4,1152]{1,0:T(4,128)S(1)}, f32[4,1152]{1,0:T(4,128)S(1)}, u32[]{:S(2)}, u32[]{:S(2)}) collective-permute-start(f32[4,1152]{1,0:T(4,128)S(1)} %get-tuple-element.12), channel_id=1, source_target_pairs={{0,2},{1,3},{2,0},{3,1},{4,6},{5,7},{6,4},{7,5},{8,10},{9,11},{10,... | collective-permute-start | bytes 55304 | tf_op jit(solution)/shard_map/ppermute | solution.py:117
  30.8 2.2 %collective-permute-done.3 = f32[4,1152]{1,0:T(4,128)S(1)} collective-permute-done((f32[4,1152]{1,0:T(4,128)S(1)}, f32[4,1152]{1,0:T(4,128)S(1)}, u32[]{:S(2)}, u32[]{:S(2)}) %collective-permute-start.3) | collective-permute-done | bytes 18464 | tf_op jit(solution)/shard_map/ppermute | solution.py:117
  33.0 0.1 collective-permute-start.4
  33.1 1.2 %collective-permute-done.4 = f32[2,1152]{1,0:T(2,128)S(1)} collective-permute-done((f32[2,1152]{1,0:T(2,128)S(1)}, f32[2,1152]{1,0:T(2,128)S(1)}, u32[]{:S(2)}, u32[]{:S(2)}) %collective-permute-start.4) | collective-permute-done | bytes 9248 | tf_op jit(solution)/shard_map/ppermute | solution.py:117
  34.2 0.1 convert_reduce_fusion
  34.4 0.7 %fusion = f32[1024,2]{0,1:T(2,128)} fusion(f32[2,1152]{1,0:T(2,128)S(1)} %select_add_fusion, f32[2]{0:T(128)S(1)} %convert_reduce_fusion), kind=kLoop, calls=%fused_computation.3 | loop fusion | flops 2048 | bytes 16392 | tf_op jit(solution)/shard_map/transpose | solution.py:144
  (5 shorter events, 0.1 us)
Async XLA Ops:
  0.7 0.7 %copy-start.2 = (s32[1024]{0:T(1024)S(1)}, s32[1024]{0:T(1024)}, u32[]{:S(2)}) copy-start(s32[1024]{0:T(1024)} %param.5) | copy-start | bytes 12292
  1.3 0.7 %copy-start.3 = (s32[64]{0:T(128)S(1)}, s32[64]{0:T(128)}, u32[]{:S(2)}) copy-start(s32[64]{0:T(128)} %param.6) | copy-start | bytes 772
  4.4 1.9 %copy-start = (bf16[1024,2048]{1,0:T(8,128)(2,1)}, bf16[1024,2048]{1,0:T(8,128)(2,1)S(1)}, u32[]{:S(2)}) copy-start(bf16[1024,2048]{1,0:T(8,128)(2,1)S(1)} %get-tuple-element.10.acts_ref) | copy-start | bytes 12582916
  6.3 6.6 %collective-permute-start = (f32[16,2176]{1,0:T(8,128)S(1)}, f32[16,2176]{1,0:T(8,128)S(1)}, u32[]{:S(2)}, u32[]{:S(2)}) collective-permute-start(f32[16,2176]{1,0:T(8,128)S(1)} %get-tuple-element.9), channel_id=1, source_target_pairs={{0,4},{4,0},{8,12},{12,8},{16,20},{20,16},{24,28},{28,24},{1,5},{5... | collective-permute-start | bytes 417800 | tf_op jit(solution)/shard_map/ppermute | solution.py:117
  13.0 5.1 %collective-permute-start.1 = (f32[16,2176]{1,0:T(8,128)S(1)}, f32[16,2176]{1,0:T(8,128)S(1)}, u32[]{:S(2)}, u32[]{:S(2)}) collective-permute-start(f32[16,2176]{1,0:T(8,128)S(1)} %add.26), channel_id=1, source_target_pairs={{0,8},{4,12},{8,0},{12,4},{16,24},{20,28},{24,16},{28,20},{1,9},{5... | collective-permute-start | bytes 417800 | tf_op jit(solution)/shard_map/ppermute | solution.py:117
  18.1 7.7 %collective-permute-start.2 = (f32[16,2176]{1,0:T(8,128)S(1)}, f32[16,2176]{1,0:T(8,128)S(1)}, u32[]{:S(2)}, u32[]{:S(2)}) collective-permute-start(f32[16,2176]{1,0:T(8,128)S(1)} %add.27.mine_ref), channel_id=1, source_target_pairs={{0,16},{4,20},{8,24},{12,28},{16,0},{20,4},{24,8},{28,12},{1,17},{... | collective-permute-start | bytes 417800 | tf_op jit(solution)/shard_map/ppermute | solution.py:117
  25.8 2.2 %copy-start.1 = (bf16[1024,2048]{1,0:T(8,128)(2,1)S(1)}, bf16[1024,2048]{1,0:T(8,128)(2,1)}, u32[]{:S(2)}) copy-start(bf16[1024,2048]{1,0:T(8,128)(2,1)} %copy-done) | copy-start | bytes 12582916
  29.2 3.8 %collective-permute-start.3 = (f32[4,1152]{1,0:T(4,128)S(1)}, f32[4,1152]{1,0:T(4,128)S(1)}, u32[]{:S(2)}, u32[]{:S(2)}) collective-permute-start(f32[4,1152]{1,0:T(4,128)S(1)} %get-tuple-element.12), channel_id=1, source_target_pairs={{0,2},{1,3},{2,0},{3,1},{4,6},{5,7},{6,4},{7,5},{8,10},{9,11},{10,... | collective-permute-start | bytes 55304 | tf_op jit(solution)/shard_map/ppermute | solution.py:117
  33.0 1.2 %collective-permute-start.4 = (f32[2,1152]{1,0:T(2,128)S(1)}, f32[2,1152]{1,0:T(2,128)S(1)}, u32[]{:S(2)}, u32[]{:S(2)}) collective-permute-start(f32[2,1152]{1,0:T(2,128)S(1)} %broadcast_select_fusion), channel_id=1, source_target_pairs={{0,1},{1,0},{2,3},{3,2},{4,5},{5,4},{6,7},{7,6},{8,9},{9,8},{10,11... | collective-permute-start | bytes 27656 | tf_op jit(solution)/shard_map/ppermute | solution.py:117

commit v2 on v1

v2 whole, which is shorter than its diff:
```python
import functools

import jax
import jax.numpy as jnp
from jax import lax
from jax.experimental import pallas as pl
from jax.experimental.pallas import tpu as pltpu
from jax.sharding import PartitionSpec as P

CAND_DEV = 1
PER_PROMPT = 16
LANES = 128
VMEM_LIMIT = 32 * 1024 * 1024

epsilon = 1e-06

VMEM = pl.BlockSpec(memory_space=pltpu.VMEM)
HBM = pl.BlockSpec(memory_space=pltpu.HBM)


def in_hbm(value):
    return pltpu.with_memory_space_constraint(value, pltpu.HBM)


def sums_kernel(
    steps, counts_ref, cand_hbm, labels_hbm, acts_hbm, sums_ref, acts_ref,
    cand_ref, labels_ref, small_sems, sems,
):
    rows, width = acts_ref.shape
    classes = sums_ref.shape[0]
    cands = classes // 2
    prompts = labels_ref.shape[1]
    tall = rows // steps

    small = [
        pltpu.make_async_copy(source, target, small_sems.at[place])
        for place, (source, target) in enumerate(
            ((cand_hbm, cand_ref), (labels_hbm, labels_ref))
        )
    ]

    def fetch(step):
        part = pl.ds(step * tall, tall)
        return pltpu.make_async_copy(acts_hbm.at[part, :], acts_ref.at[part, :], sems.at[step])

    for copy in small:
        copy.start()
    for step in range(steps):
        fetch(step).start()

    prompt_ids = lax.broadcasted_iota(jnp.int32, (prompts, rows), 0)
    prompt_of = lax.broadcasted_iota(jnp.int32, (prompts, rows), 1) // PER_PROMPT
    spread = jnp.where(prompt_ids == prompt_of, 1.0, 0.0).astype(jnp.bfloat16)
    wanted = lax.broadcasted_iota(jnp.int32, (classes, rows), 0)
    row_prompt = lax.broadcasted_iota(jnp.int32, (1, rows), 1) // PER_PROMPT
    for copy in small:
        copy.wait()
    labels = jnp.broadcast_to(labels_ref[...].astype(jnp.float32), (8, prompts))
    row_class = jnp.dot(labels.astype(jnp.bfloat16), spread, preferred_element_type=jnp.float32)[:1]
    slot = jnp.where(row_class == 1.0, cand_ref[...], cand_ref[...] + cands)
    slot = jnp.where(row_prompt < counts_ref[0], slot, -1)
    member_float = jnp.where(wanted == slot, 1.0, 0.0)
    member = member_float.astype(jnp.bfloat16)
    tally = jnp.sum(member_float, axis=1, keepdims=True)
    sums_ref[:, width:] = jnp.broadcast_to(tally, (classes, LANES))

    total = None
    for step in range(steps):
        fetch(step).wait()
        piece = jnp.dot(
            member[:, step * tall : (step + 1) * tall],
            acts_ref[step * tall : (step + 1) * tall, :],
            preferred_element_type=jnp.float32,
        )
        total = piece if total is None else total + piece
    sums_ref[:, :width] = total


def class_sums(activations, cand_index, labels, counts, classes, steps=8):
    rows, width = activations.shape
    prompts = labels.shape[0]
    return pl.pallas_call(
        functools.partial(sums_kernel, steps),
        out_shape=(
            jax.ShapeDtypeStruct((classes, width + LANES), jnp.float32),
            pltpu.VMEM((rows, width), activations.dtype),
        ),
        in_specs=[pl.BlockSpec(memory_space=pltpu.SMEM)] + [HBM] * 3,
        out_specs=(VMEM, VMEM),
        scratch_shapes=[
            pltpu.VMEM((1, rows), jnp.int32),
            pltpu.VMEM((1, prompts), jnp.int32),
            pltpu.SemaphoreType.DMA((2,)),
            pltpu.SemaphoreType.DMA((steps,)),
        ],
        compiler_params=pltpu.CompilerParams(vmem_limit_bytes=VMEM_LIMIT),
        name="class_sums",
    )(
        counts,
        in_hbm(cand_index.reshape(1, rows)),
        in_hbm(labels.reshape(1, prompts)),
        in_hbm(activations),
    )


def project_kernel(mine_ref, other_ref, acts_ref, keep_ref, *send_refs):
    rows, width = acts_ref.shape
    cands = mine_ref.shape[0] // 2
    parts = len(send_refs) + 1
    part = cands // parts
    place = lax.axis_index("feat")
    total = mine_ref[...] + other_ref[...]
    tally = jnp.maximum(total[:, width : width + 1], 1.0)
    harmful_mean = total[:cands, :width] / tally[:cands]
    harmless_mean = total[cands:, :width] / tally[cands:]
    raw_dir = (harmful_mean - harmless_mean).astype(jnp.bfloat16)
    squares = jnp.sum(jnp.square(raw_dir.astype(jnp.float32)), axis=1, keepdims=True)
    squares = jnp.broadcast_to(squares, (cands, LANES))
    plain = lax.dot_general(
        raw_dir, acts_ref[...], (((1,), (1,)), ((), ())), preferred_element_type=jnp.float32
    )
    for step, out_ref in enumerate((keep_ref,) + send_refs):
        for value, columns in ((plain, slice(0, rows)), (squares, slice(rows, rows + LANES))):
            chosen = value[:part]
            for block in range(1, parts):
                mine = place == block ^ step
                chosen = jnp.where(mine, value[block * part : (block + 1) * part], chosen)
            out_ref[:, columns] = chosen


def project(mine, other, acts):
    rows = acts.shape[0]
    parts = lax.axis_size("feat")
    part = jax.ShapeDtypeStruct((mine.shape[0] // 2 // parts, rows + LANES), jnp.float32)
    return pl.pallas_call(
        project_kernel,
        out_shape=(part,) * parts,
        in_specs=[VMEM] * 3,
        out_specs=(VMEM,) * parts,
        compiler_params=pltpu.CompilerParams(vmem_limit_bytes=VMEM_LIMIT),
        name="project",
    )(mine, other, pltpu.with_memory_space_constraint(acts, pltpu.VMEM))


def scale_kernel(*refs):
    *share_refs, scores_ref = refs
    rows = scores_ref.shape[1]
    total = share_refs[0][...]
    for ref in share_refs[1:]:
        total = total + ref[...]
    inv_norm = lax.rsqrt(total[:, rows : rows + 1] + epsilon).astype(jnp.bfloat16)
    scores_ref[...] = total[:, :rows] * inv_norm.astype(jnp.float32)


def scale(shares):
    part, columns = shares[0].shape
    return pl.pallas_call(
        scale_kernel,
        out_shape=jax.ShapeDtypeStruct((part, columns - LANES), jnp.float32),
        in_specs=[VMEM] * len(shares),
        out_specs=VMEM,
        compiler_params=pltpu.CompilerParams(vmem_limit_bytes=VMEM_LIMIT),
        name="scale",
    )(*shares)


def dp_trade(value, step):
    dp, feat = lax.axis_size("dp"), lax.axis_size("feat")
    bits = [1 << b for b in range(dp.bit_length() - 1)]
    bits = bits[:1] + bits[:0:-1]
    pairs = []
    for d in range(dp):
        for f in range(feat):
            bit = bits[(step + f % 2) % len(bits)]
            pairs.append((d * feat + f, (d ^ bit) * feat + f))
    return lax.ppermute(value, ("dp", "feat"), pairs)


def feat_trade(value, bits):
    return lax.ppermute(value, "feat", [(f, f ^ bits) for f in range(lax.axis_size("feat"))])


def per_device(activations, cand_index, labels, counts):
    dp, feat = lax.axis_size("dp"), lax.axis_size("feat")
    sums, acts = class_sums(activations, cand_index, labels, counts, 2 * CAND_DEV * dp)
    rounds = dp.bit_length() - 1
    for step in range(rounds - 1):
        sums = sums + dp_trade(sums, step)
    keep, *sends = project(sums, dp_trade(sums, rounds - 1), acts)
    shares = [feat_trade(sends[bits - 1], bits) for bits in range(feat - 1, 0, -1)]
    return scale([keep] + shares).T


def solution(mesh):
    return jax.shard_map(
        per_device,
        mesh=mesh,
        in_specs=(P("dp", "feat"), P("dp"), P("dp"), P("dp")),
        out_specs=P("dp", "feat"),
        check_vma=False,
    )
```

time: 35.2 us -> 28.1 us (0.80)
  local copies, waits for them, and re-layouts: 5.45 us -> 0 us
  waiting for transfers between devices: 15.1 us -> 11.2 us
  starting transfers between devices: 9.37 us -> 11.3 us
  Pallas kernels: 3.6 us -> 4.69 us
  other arithmetic: 0.86 us -> 0.03 us
    unnamed x8 -> x0, local copies, waits for them, and re-layouts: 5.45 us -> none
    ppermute x5 -> x6, waiting for transfers between devices: 15.1 us -> 11.2 us  [the longest x3 9.34 us: dp_trade(): return lax.ppermute(value, ('dp', 'feat'), pairs)]
    ppermute x5 -> x6, starting transfers between devices: 9.37 us -> 11.3 us  [the longest x3 9.35 us: dp_trade(): return lax.ppermute(value, ('dp', 'feat'), pairs)]
    pallas_call x1 -> x2, Pallas kernels: 1.2 us -> 1.91 us  [the longest x1 1.22 us: project(): pl.pallas_call(project_kernel, out_shape=(part,) * parts, in_specs=[VMEM]...]
    transpose x1 -> x0, other arithmetic: 0.68 us -> none  [per_device(): return (keep[:, :rows] * inv_norm.astype(jnp.float32)).T]
    pallas_call x1, Pallas kernels: 2.4 us -> 2.79 us  [class_sums(): pl.pallas_call(functools.partial(sums_kernel, steps), out_shape=(jax.Shap...]
  transfers between devices with their start and end apart: 5 -> 6, of which waited for: 5 -> 5; matrix products, arithmetic and copies ran while one was open for 0% -> 0% of each run, Pallas kernels for 0% -> 0%
where the time goes in v2:
time: 28.1 us; the launch traced here: 27.9 us
  starting transfers between devices  11.3 us (40%)
  waiting for transfers between devices  11.2 us (40%)
  Pallas kernels  4.69 us (17%)
  between operations  0.69 us (2%)
    ppermute x3, starting transfers between devices, dp_trade(): return lax.ppermute(value, ('dp', 'feat'), pairs)  9.35 us
    ppermute x3, waiting for transfers between devices, dp_trade(): return lax.ppermute(value, ('dp', 'feat'), pairs)  9.34 us
    pallas_call x1, Pallas kernels, class_sums(): pl.pallas_call(functools.partial(sums_kernel, steps), out_shape=(jax.Shap...  2.79 us
    ppermute x3, starting transfers between devices, feat_trade(): lax.ppermute(value, 'feat', [(f, f ^ bits) for f in range(lax.axis_size('...  1.92 us
    ppermute x3, waiting for transfers between devices, feat_trade(): lax.ppermute(value, 'feat', [(f, f ^ bits) for f in range(lax.axis_size('...  1.88 us
    pallas_call x1, Pallas kernels, project(): pl.pallas_call(project_kernel, out_shape=(part,) * parts, in_specs=[VMEM]...  1.22 us
    pallas_call x1, Pallas kernels, scale(): pl.pallas_call(scale_kernel, out_shape=jax.ShapeDtypeStruct((part, column...  0.68 us
  transfers between devices with their start and end apart: 6, of which 5 were waited for; matrix products, arithmetic and copies ran while one was open for 0% of the time, Pallas kernels for 0%

profile of v2, /device:TPU:0, one launch (start us, length us, event | category | flops | bytes accessed | tf_op | source)
XLA Modules:
  0.0 27.9 jit_solution(6934284125840602294)
XLA Ops:
  0.7 2.8 %class_sums.1 = (f32[16,2176]{1,0:T(8,128)S(1)}, bf16[1024,2048]{1,0:T(8,128)(2,1)S(1)}) custom-call(s32[1]{0:T(128)S(6)} %copy.5.counts_ref, s32[1,1024]{1,0:T(1,128)} %bitcast.3, s32[1,64]{1,0:T(1,128)} %bitcast.4, bf16[1024,2048]{1,0:T(8,128)(2,1)} %acts_hbm.1), custom_call_target="tpu_custom_call" | custom-call | tf_op jit(solution)/shard_map/class_sums/pallas_call | solution.py:82
  3.4 3.0 %collective-permute-start = (f32[16,2176]{1,0:T(8,128)S(1)}, f32[16,2176]{1,0:T(8,128)S(1)}, u32[]{:S(2)}, u32[]{:S(2)}) collective-permute-start(f32[16,2176]{1,0:T(8,128)S(1)} %get-tuple-element.11), channel_id=1, source_target_pairs={{0,4},{1,17},{2,6},{3,19},{4,0},{5,21},{6,2},{7,23},{8,12},{9,25},... | collective-permute-start | bytes 417800 | tf_op jit(solution)/shard_map/ppermute | solution.py:176
  6.5 3.0 %collective-permute-done = f32[16,2176]{1,0:T(8,128)S(1)} collective-permute-done((f32[16,2176]{1,0:T(8,128)S(1)}, f32[16,2176]{1,0:T(8,128)S(1)}, u32[]{:S(2)}, u32[]{:S(2)}) %collective-permute-start) | collective-permute-done | bytes 139296 | tf_op jit(solution)/shard_map/ppermute | solution.py:176
  9.5 3.2 %collective-permute-start.1 = (f32[16,2176]{1,0:T(8,128)S(1)}, f32[16,2176]{1,0:T(8,128)S(1)}, u32[]{:S(2)}, u32[]{:S(2)}) collective-permute-start(f32[16,2176]{1,0:T(8,128)S(1)} %add.6), channel_id=1, source_target_pairs={{0,16},{1,9},{2,18},{3,11},{4,20},{5,13},{6,22},{7,15},{8,24},{9,1... | collective-permute-start | bytes 417800 | tf_op jit(solution)/shard_map/ppermute | solution.py:176
  12.7 3.3 %collective-permute-done.1 = f32[16,2176]{1,0:T(8,128)S(1)} collective-permute-done((f32[16,2176]{1,0:T(8,128)S(1)}, f32[16,2176]{1,0:T(8,128)S(1)}, u32[]{:S(2)}, u32[]{:S(2)}) %collective-permute-start.1) | collective-permute-done | bytes 139296 | tf_op jit(solution)/shard_map/ppermute | solution.py:176
  16.0 3.2 %collective-permute-start.2 = (f32[16,2176]{1,0:T(8,128)S(1)}, f32[16,2176]{1,0:T(8,128)S(1)}, u32[]{:S(2)}, u32[]{:S(2)}) collective-permute-start(f32[16,2176]{1,0:T(8,128)S(1)} %add.7.mine_ref), channel_id=1, source_target_pairs={{0,8},{1,5},{2,10},{3,7},{4,12},{5,1},{6,14},{7,3},{8,0},{9,13},{1... | collective-permute-start | bytes 417800 | tf_op jit(solution)/shard_map/ppermute | solution.py:176
  19.2 3.0 %collective-permute-done.2.other_ref = f32[16,2176]{1,0:T(8,128)S(1)} collective-permute-done((f32[16,2176]{1,0:T(8,128)S(1)}, f32[16,2176]{1,0:T(8,128)S(1)}, u32[]{:S(2)}, u32[]{:S(2)}) %collective-permute-start.2) | collective-permute-done | bytes 139296 | tf_op jit(solution)/shard_map/ppermute | solution.py:176
  22.2 1.2 %project.1 = (f32[2,1152]{1,0:T(2,128)S(1)}, f32[2,1152]{1,0:T(2,128)S(1)}, f32[2,1152]{1,0:T(2,128)S(1)}, f32[2,1152]{1,0:T(2,128)S(1)}) custom-call(f32[16,2176]{1,0:T(8,128)S(1)} %add.7.mine_ref, f32[16,2176]{1,0:T(8,128)S(1)} %collective-permute-done.2.other_ref, bf16[1024,2048]{1,0:T(8,128)(2,1)S(1)} %get-tuple-element.12.acts_ref), custom_call_target="tpu_custom_call" | custom-call | tf_op jit(solution)/shard_map/project/pallas_call | solution.py:135
  23.4 0.1 collective-permute-start.3
  23.5 1.6 %collective-permute-start.4 = (f32[2,1152]{1,0:T(2,128)S(1)}, f32[2,1152]{1,0:T(2,128)S(1)}, u32[]{:S(2)}, u32[]{:S(2)}) collective-permute-start(f32[2,1152]{1,0:T(2,128)S(1)} %get-tuple-element.15), channel_id=1, source_target_pairs={{0,2},{1,3},{2,0},{3,1},{4,6},{5,7},{6,4},{7,5},{8,10},{9,11},{10,... | collective-permute-start | bytes 27656 | tf_op jit(solution)/shard_map/ppermute | solution.py:180
  25.1 0.3 %collective-permute-start.5 = (f32[2,1152]{1,0:T(2,128)S(1)}, f32[2,1152]{1,0:T(2,128)S(1)}, u32[]{:S(2)}, u32[]{:S(2)}) collective-permute-start(f32[2,1152]{1,0:T(2,128)S(1)} %get-tuple-element.16), channel_id=1, source_target_pairs={{0,1},{1,0},{2,3},{3,2},{4,5},{5,4},{6,7},{7,6},{8,9},{9,8},{10,11... | collective-permute-start | bytes 27656 | tf_op jit(solution)/shard_map/ppermute | solution.py:180
  25.3 1.3 %collective-permute-done.3.refs_1_ = f32[2,1152]{1,0:T(2,128)S(1)} collective-permute-done((f32[2,1152]{1,0:T(2,128)S(1)}, f32[2,1152]{1,0:T(2,128)S(1)}, u32[]{:S(2)}, u32[]{:S(2)}) %collective-permute-start.3) | collective-permute-done | bytes 9248 | tf_op jit(solution)/shard_map/ppermute | solution.py:180
  26.6 0.6 %collective-permute-done.4.refs_2_ = f32[2,1152]{1,0:T(2,128)S(1)} collective-permute-done((f32[2,1152]{1,0:T(2,128)S(1)}, f32[2,1152]{1,0:T(2,128)S(1)}, u32[]{:S(2)}, u32[]{:S(2)}) %collective-permute-start.4) | collective-permute-done | bytes 9248 | tf_op jit(solution)/shard_map/ppermute | solution.py:180
  27.2 0.0 collective-permute-done.5.refs_3_
  27.2 0.7 %scale.1 = f32[2,1024]{1,0:T(2,128)} custom-call(f32[2,1152]{1,0:T(2,128)S(1)} %get-tuple-element.13.refs_0_, f32[2,1152]{1,0:T(2,128)S(1)} %collective-permute-done.3.refs_1_, f32[2,1152]{1,0:T(2,128)S(1)} %collective-permute-done.4.refs_2_, f32[2,1152]{1,0:T(2,128)S(1)} %collective-permute-done.5.refs_3_), custom_call_target="tpu_custom_call" | custom-call | tf_op jit(solution)/shard_map/scale/pallas_call | solution.py:157
  (2 shorter events, 0.0 us)
Async XLA Ops:
  3.4 6.1 %collective-permute-start = (f32[16,2176]{1,0:T(8,128)S(1)}, f32[16,2176]{1,0:T(8,128)S(1)}, u32[]{:S(2)}, u32[]{:S(2)}) collective-permute-start(f32[16,2176]{1,0:T(8,128)S(1)} %get-tuple-element.11), channel_id=1, source_target_pairs={{0,4},{1,17},{2,6},{3,19},{4,0},{5,21},{6,2},{7,23},{8,12},{9,25},... | collective-permute-start | bytes 417800 | tf_op jit(solution)/shard_map/ppermute | solution.py:176
  9.5 6.4 %collective-permute-start.1 = (f32[16,2176]{1,0:T(8,128)S(1)}, f32[16,2176]{1,0:T(8,128)S(1)}, u32[]{:S(2)}, u32[]{:S(2)}) collective-permute-start(f32[16,2176]{1,0:T(8,128)S(1)} %add.6), channel_id=1, source_target_pairs={{0,16},{1,9},{2,18},{3,11},{4,20},{5,13},{6,22},{7,15},{8,24},{9,1... | collective-permute-start | bytes 417800 | tf_op jit(solution)/shard_map/ppermute | solution.py:176
  16.0 6.2 %collective-permute-start.2 = (f32[16,2176]{1,0:T(8,128)S(1)}, f32[16,2176]{1,0:T(8,128)S(1)}, u32[]{:S(2)}, u32[]{:S(2)}) collective-permute-start(f32[16,2176]{1,0:T(8,128)S(1)} %add.7.mine_ref), channel_id=1, source_target_pairs={{0,8},{1,5},{2,10},{3,7},{4,12},{5,1},{6,14},{7,3},{8,0},{9,13},{1... | collective-permute-start | bytes 417800 | tf_op jit(solution)/shard_map/ppermute | solution.py:176
  23.4 3.2 %collective-permute-start.3 = (f32[2,1152]{1,0:T(2,128)S(1)}, f32[2,1152]{1,0:T(2,128)S(1)}, u32[]{:S(2)}, u32[]{:S(2)}) collective-permute-start(f32[2,1152]{1,0:T(2,128)S(1)} %get-tuple-element.14), channel_id=1, source_target_pairs={{0,3},{1,2},{2,1},{3,0},{4,7},{5,6},{6,5},{7,4},{8,11},{9,10},{10,... | collective-permute-start | bytes 27656 | tf_op jit(solution)/shard_map/ppermute | solution.py:180
  23.5 3.7 %collective-permute-start.4 = (f32[2,1152]{1,0:T(2,128)S(1)}, f32[2,1152]{1,0:T(2,128)S(1)}, u32[]{:S(2)}, u32[]{:S(2)}) collective-permute-start(f32[2,1152]{1,0:T(2,128)S(1)} %get-tuple-element.15), channel_id=1, source_target_pairs={{0,2},{1,3},{2,0},{3,1},{4,6},{5,7},{6,4},{7,5},{8,10},{9,11},{10,... | collective-permute-start | bytes 27656 | tf_op jit(solution)/shard_map/ppermute | solution.py:180
  25.1 2.2 %collective-permute-start.5 = (f32[2,1152]{1,0:T(2,128)S(1)}, f32[2,1152]{1,0:T(2,128)S(1)}, u32[]{:S(2)}, u32[]{:S(2)}) collective-permute-start(f32[2,1152]{1,0:T(2,128)S(1)} %get-tuple-element.16), channel_id=1, source_target_pairs={{0,1},{1,0},{2,3},{3,2},{4,5},{5,4},{6,7},{7,6},{8,9},{9,8},{10,11... | collective-permute-start | bytes 27656 | tf_op jit(solution)/shard_map/ppermute | solution.py:180

commit v3 on v2

--- a/solution.py
+++ b/solution.py
@@ -22,12 +22,17 @@
     return pltpu.with_memory_space_constraint(value, pltpu.HBM)
 
 
+def in_vmem(value):
+    return pltpu.with_memory_space_constraint(value, pltpu.VMEM)
+
+
 def sums_kernel(
-    steps, counts_ref, cand_hbm, labels_hbm, acts_hbm, sums_ref, acts_ref,
+    steps, counts_ref, cand_hbm, labels_hbm, acts_hbm, sums_ref, member_ref, acts_ref,
     cand_ref, labels_ref, small_sems, sems,
 ):
-    rows, width = acts_ref.shape
+    rows = acts_ref.shape[0]
     classes = sums_ref.shape[0]
+    first = sums_ref.shape[1] - LANES
     cands = classes // 2
     prompts = labels_ref.shape[1]
     tall = rows // steps
@@ -61,32 +66,34 @@
     slot = jnp.where(row_prompt < counts_ref[0], slot, -1)
     member_float = jnp.where(wanted == slot, 1.0, 0.0)
     member = member_float.astype(jnp.bfloat16)
+    member_ref[...] = member
     tally = jnp.sum(member_float, axis=1, keepdims=True)
-    sums_ref[:, width:] = jnp.broadcast_to(tally, (classes, LANES))
+    sums_ref[:, first:] = jnp.broadcast_to(tally, (classes, LANES))
 
     total = None
     for step in range(steps):
         fetch(step).wait()
         piece = jnp.dot(
             member[:, step * tall : (step + 1) * tall],
-            acts_ref[step * tall : (step + 1) * tall, :],
+            acts_ref[step * tall : (step + 1) * tall, :first],
             preferred_element_type=jnp.float32,
         )
         total = piece if total is None else total + piece
-    sums_ref[:, :width] = total
-
-
-def class_sums(activations, cand_index, labels, counts, classes, steps=8):
+    sums_ref[:, :first] = total
+
+
+def class_sums(activations, cand_index, labels, counts, classes, first, steps=8):
     rows, width = activations.shape
     prompts = labels.shape[0]
     return pl.pallas_call(
         functools.partial(sums_kernel, steps),
         out_shape=(
-            jax.ShapeDtypeStruct((classes, width + LANES), jnp.float32),
+            jax.ShapeDtypeStruct((classes, first + LANES), jnp.float32),
+            pltpu.VMEM((classes, rows), jnp.bfloat16),
             pltpu.VMEM((rows, width), activations.dtype),
         ),
         in_specs=[pl.BlockSpec(memory_space=pltpu.SMEM)] + [HBM] * 3,
-        out_specs=(VMEM, VMEM),
+        out_specs=(VMEM,) * 3,
         scratch_shapes=[
             pltpu.VMEM((1, rows), jnp.int32),
             pltpu.VMEM((1, prompts), jnp.int32),
@@ -103,22 +110,79 @@
     )
 
 
-def project_kernel(mine_ref, other_ref, acts_ref, keep_ref, *send_refs):
+def rest_kernel(member_ref, acts_ref, sums_ref):
+    first = acts_ref.shape[1] - sums_ref.shape[1]
+    sums_ref[...] = jnp.dot(
+        member_ref[...], acts_ref[:, first:], preferred_element_type=jnp.float32
+    )
+
+
+def rest_sums(member, acts, first):
+    rows, width = acts.shape
+    classes = member.shape[0]
+    return pl.pallas_call(
+        rest_kernel,
+        out_shape=jax.ShapeDtypeStruct((classes, width - first), jnp.float32),
+        in_specs=[VMEM] * 2,
+        out_specs=VMEM,
+        cost_estimate=pl.CostEstimate(
+            flops=2 * classes * rows * (width - first), bytes_accessed=2 * rows * width, transcendentals=0
+        ),
+        compiler_params=pltpu.CompilerParams(vmem_limit_bytes=VMEM_LIMIT),
+        name="rest_sums",
+    )(in_vmem(member), in_vmem(acts))
+
+
+def directions(total, tally):
+    cands = total.shape[0] // 2
+    harmful_mean = total[:cands] / tally[:cands]
+    harmless_mean = total[cands:] / tally[cands:]
+    raw_dir = (harmful_mean - harmless_mean).astype(jnp.bfloat16)
+    return raw_dir, jnp.sum(jnp.square(raw_dir.astype(jnp.float32)), axis=1, keepdims=True)
+
+
+def project_kernel(mine_ref, other_ref, acts_ref, shares_ref, tally_ref):
+    rows = acts_ref.shape[0]
+    first = mine_ref.shape[1] - LANES
+    total = mine_ref[...] + other_ref[...]
+    tally = jnp.maximum(total[:, first:], 1.0)
+    tally_ref[...] = tally
+    raw_dir, squares = directions(total[:, :first], tally[:, :1])
+    shares_ref[:, :rows] = lax.dot_general(
+        raw_dir, acts_ref[:, :first], (((1,), (1,)), ((), ())), preferred_element_type=jnp.float32
+    )
+    shares_ref[:, rows:] = jnp.broadcast_to(squares, (squares.shape[0], LANES))
+
+
+def project(mine, other, acts):
+    rows = acts.shape[0]
+    classes = mine.shape[0]
+    return pl.pallas_call(
+        project_kernel,
+        out_shape=(
+            jax.ShapeDtypeStruct((classes // 2, rows + LANES), jnp.float32),
+            jax.ShapeDtypeStruct((classes, LANES), jnp.float32),
+        ),
+        in_specs=[VMEM] * 3,
+        out_specs=(VMEM,) * 2,
+        compiler_params=pltpu.CompilerParams(vmem_limit_bytes=VMEM_LIMIT),
+        name="project",
+    )(mine, other, in_vmem(acts))
+
+
+def project_rest_kernel(mine_ref, other_ref, tally_ref, shares_ref, acts_ref, keep_ref, *send_refs):
     rows, width = acts_ref.shape
+    first = width - mine_ref.shape[1]
     cands = mine_ref.shape[0] // 2
     parts = len(send_refs) + 1
     part = cands // parts
     place = lax.axis_index("feat")
-    total = mine_ref[...] + other_ref[...]
-    tally = jnp.maximum(total[:, width : width + 1], 1.0)
-    harmful_mean = total[:cands, :width] / tally[:cands]
-    harmless_mean = total[cands:, :width] / tally[cands:]
-    raw_dir = (harmful_mean - harmless_mean).astype(jnp.bfloat16)
-    squares = jnp.sum(jnp.square(raw_dir.astype(jnp.float32)), axis=1, keepdims=True)
-    squares = jnp.broadcast_to(squares, (cands, LANES))
+    raw_dir, squares = directions(mine_ref[...] + other_ref[...], tally_ref[:, :1])
     plain = lax.dot_general(
-        raw_dir, acts_ref[...], (((1,), (1,)), ((), ())), preferred_element_type=jnp.float32
-    )
+        raw_dir, acts_ref[:, first:], (((1,), (1,)), ((), ())), preferred_element_type=jnp.float32
+    )
+    plain = plain + shares_ref[:, :rows]
+    squares = squares + shares_ref[:, rows:]
     for step, out_ref in enumerate((keep_ref,) + send_refs):
         for value, columns in ((plain, slice(0, rows)), (squares, slice(rows, rows + LANES))):
             chosen = value[:part]
@@ -128,18 +192,18 @@
             out_ref[:, columns] = chosen
 
 
-def project(mine, other, acts):
+def project_rest(mine, other, tally, shares, acts):
     rows = acts.shape[0]
     parts = lax.axis_size("feat")
     part = jax.ShapeDtypeStruct((mine.shape[0] // 2 // parts, rows + LANES), jnp.float32)
     return pl.pallas_call(
-        project_kernel,
+        project_rest_kernel,
         out_shape=(part,) * parts,
-        in_specs=[VMEM] * 3,
+        in_specs=[VMEM] * 5,
         out_specs=(VMEM,) * parts,
         compiler_params=pltpu.CompilerParams(vmem_limit_bytes=VMEM_LIMIT),
-        name="project",
-    )(mine, other, pltpu.with_memory_space_constraint(acts, pltpu.VMEM))
+        name="project_rest",
+    )(mine, other, tally, shares, in_vmem(acts))
 
 
 def scale_kernel(*refs):
@@ -182,11 +246,17 @@
 
 def per_device(activations, cand_index, labels, counts):
     dp, feat = lax.axis_size("dp"), lax.axis_size("feat")
-    sums, acts = class_sums(activations, cand_index, labels, counts, 2 * CAND_DEV * dp)
+    first = activations.shape[1] // 2
+    sums, member, acts = class_sums(
+        activations, cand_index, labels, counts, 2 * CAND_DEV * dp, first
+    )
+    rest = rest_sums(member, acts, first)
     rounds = dp.bit_length() - 1
     for step in range(rounds - 1):
         sums = sums + dp_trade(sums, step)
-    keep, *sends = project(sums, dp_trade(sums, rounds - 1), acts)
+        rest = rest + dp_trade(rest, step)
+    shares, tally = project(sums, dp_trade(sums, rounds - 1), acts)
+    keep, *sends = project_rest(rest, dp_trade(rest, rounds - 1), tally, shares, acts)
     shares = [feat_trade(sends[bits - 1], bits) for bits in range(feat - 1, 0, -1)]
     return scale([keep] + shares).T
 

time: 28.1 us -> 26.6 us (0.947)
  waiting for transfers between devices: 11.2 us -> 6.67 us
  starting transfers between devices: 11.3 us -> 14.2 us
    ppermute x3 -> x6, waiting for transfers between devices: 9.34 us -> 4.78 us  [dp_trade(): return lax.ppermute(value, ('dp', 'feat'), pairs)]
    ppermute x3 -> x6, starting transfers between devices: 9.35 us -> 12.3 us  [dp_trade(): return lax.ppermute(value, ('dp', 'feat'), pairs)]
    pallas_call x1 -> x3, Pallas kernels: 1.22 us -> 1.71 us  [the longest x1 0.68 us: project_rest(): pl.pallas_call(project_rest_kernel, out_shape=(part,) * parts, in_specs=[...]
    pallas_call x1, Pallas kernels: 2.79 us -> 2.5 us  [class_sums(): pl.pallas_call(functools.partial(sums_kernel, steps), out_shape=(jax.Shap...]
  transfers between devices with their start and end apart: 6 -> 9, of which waited for: 5 -> 7; matrix products, arithmetic and copies ran while one was open for 0% -> 0% of each run, Pallas kernels for 0% -> 4%
where the time goes in v3:
time: 26.6 us; the launch traced here: 26.5 us
  starting transfers between devices  14.2 us (53%)
  waiting for transfers between devices  6.67 us (25%)
  Pallas kernels  4.9 us (18%)
  between operations  0.7 us (3%)
    ppermute x6, starting transfers between devices, dp_trade(): return lax.ppermute(value, ('dp', 'feat'), pairs)  12.3 us
    ppermute x6, waiting for transfers between devices, dp_trade(): return lax.ppermute(value, ('dp', 'feat'), pairs)  4.78 us
    pallas_call x1, Pallas kernels, class_sums(): pl.pallas_call(functools.partial(sums_kernel, steps), out_shape=(jax.Shap...  2.5 us
    ppermute x3, starting transfers between devices, feat_trade(): lax.ppermute(value, 'feat', [(f, f ^ bits) for f in range(lax.axis_size('...  1.92 us
    ppermute x3, waiting for transfers between devices, feat_trade(): lax.ppermute(value, 'feat', [(f, f ^ bits) for f in range(lax.axis_size('...  1.88 us
    pallas_call x1, Pallas kernels, scale(): pl.pallas_call(scale_kernel, out_shape=jax.ShapeDtypeStruct((part, column...  0.68 us
    pallas_call x1, Pallas kernels, project_rest(): pl.pallas_call(project_rest_kernel, out_shape=(part,) * parts, in_specs=[...  0.68 us
    pallas_call x1, Pallas kernels, project(): pl.pallas_call(project_kernel, out_shape=(jax.ShapeDtypeStruct((classes /...  0.65 us
  transfers between devices with their start and end apart: 9, of which 7 were waited for; matrix products, arithmetic and copies ran while one was open for 0% of the time, Pallas kernels for 4%

profile of v3, /device:TPU:0, one launch (start us, length us, event | category | flops | bytes accessed | tf_op | source)
XLA Modules:
  0.0 26.5 jit_solution(2870495059843384727)
XLA Ops:
  0.7 2.5 %class_sums.1 = (f32[16,1152]{1,0:T(8,128)S(1)}, bf16[16,1024]{1,0:T(8,128)(2,1)S(1)}, bf16[1024,2048]{1,0:T(8,128)(2,1)S(1)}) custom-call(s32[1]{0:T(128)S(6)} %copy.5.counts_ref, s32[1,1024]{1,0:T(1,128)} %bitcast.3, s32[1,64]{1,0:T(1,128)} %bitcast.4, bf16[1024,2048]{1,0:T(8,128)(2,1)} %acts_hbm.1), custom_call_target="tpu_custom_call" | custom-call | tf_op jit(solution)/shard_map/class_sums/pallas_call | solution.py:88
  3.2 3.0 %collective-permute-start.3 = (f32[16,1152]{1,0:T(8,128)S(1)}, f32[16,1152]{1,0:T(8,128)S(1)}, u32[]{:S(2)}, u32[]{:S(2)}) collective-permute-start(f32[16,1152]{1,0:T(8,128)S(1)} %get-tuple-element.16), channel_id=1, source_target_pairs={{0,4},{1,17},{2,6},{3,19},{4,0},{5,21},{6,2},{7,23},{8,12},{9,25},... | collective-permute-start | bytes 221192 | tf_op jit(solution)/shard_map/ppermute | solution.py:240
  6.2 0.4 %rest_sums.1 = f32[16,1024]{1,0:T(8,128)S(1)} custom-call(bf16[16,1024]{1,0:T(8,128)(2,1)S(1)} %get-tuple-element.14.member_ref, bf16[1024,2048]{1,0:T(8,128)(2,1)S(1)} %get-tuple-element.15.acts_ref), custom_call_target="tpu_custom_call" | custom-call | flops 33554432 | bytes 4194304 | tf_op jit(solution)/shard_map/rest_sums/pallas_call | solution.py:123
  6.6 0.0 collective-permute-start
  6.6 1.9 %collective-permute-done.3 = f32[16,1152]{1,0:T(8,128)S(1)} collective-permute-done((f32[16,1152]{1,0:T(8,128)S(1)}, f32[16,1152]{1,0:T(8,128)S(1)}, u32[]{:S(2)}, u32[]{:S(2)}) %collective-permute-start.3) | collective-permute-done | bytes 73760 | tf_op jit(solution)/shard_map/ppermute | solution.py:240
  8.5 3.2 %collective-permute-start.4 = (f32[16,1152]{1,0:T(8,128)S(1)}, f32[16,1152]{1,0:T(8,128)S(1)}, u32[]{:S(2)}, u32[]{:S(2)}) collective-permute-start(f32[16,1152]{1,0:T(8,128)S(1)} %add.14), channel_id=1, source_target_pairs={{0,16},{1,9},{2,18},{3,11},{4,20},{5,13},{6,22},{7,15},{8,24},{9,1... | collective-permute-start | bytes 221192 | tf_op jit(solution)/shard_map/ppermute | solution.py:240
  11.7 0.0 collective-permute-done
  11.7 1.8 %collective-permute-start.1 = (f32[16,1024]{1,0:T(8,128)S(1)}, f32[16,1024]{1,0:T(8,128)S(1)}, u32[]{:S(2)}, u32[]{:S(2)}) collective-permute-start(f32[16,1024]{1,0:T(8,128)S(1)} %add.12), channel_id=1, source_target_pairs={{0,16},{1,9},{2,18},{3,11},{4,20},{5,13},{6,22},{7,15},{8,24},{9,1... | collective-permute-start | bytes 196616 | tf_op jit(solution)/shard_map/ppermute | solution.py:240
  13.5 0.6 %collective-permute-done.4 = f32[16,1152]{1,0:T(8,128)S(1)} collective-permute-done((f32[16,1152]{1,0:T(8,128)S(1)}, f32[16,1152]{1,0:T(8,128)S(1)}, u32[]{:S(2)}, u32[]{:S(2)}) %collective-permute-start.4) | collective-permute-done | bytes 73760 | tf_op jit(solution)/shard_map/ppermute | solution.py:240
  14.2 2.6 %collective-permute-start.5 = (f32[16,1152]{1,0:T(8,128)S(1)}, f32[16,1152]{1,0:T(8,128)S(1)}, u32[]{:S(2)}, u32[]{:S(2)}) collective-permute-start(f32[16,1152]{1,0:T(8,128)S(1)} %add.15.mine_ref), channel_id=1, source_target_pairs={{0,8},{1,5},{2,10},{3,7},{4,12},{5,1},{6,14},{7,3},{8,0},{9,13},{1... | collective-permute-start | bytes 221192 | tf_op jit(solution)/shard_map/ppermute | solution.py:240
  16.7 0.2 collective-permute-done.1
  17.0 1.6 %collective-permute-start.2 = (f32[16,1024]{1,0:T(8,128)S(1)}, f32[16,1024]{1,0:T(8,128)S(1)}, u32[]{:S(2)}, u32[]{:S(2)}) collective-permute-start(f32[16,1024]{1,0:T(8,128)S(1)} %add.13.mine_ref), channel_id=1, source_target_pairs={{0,8},{1,5},{2,10},{3,7},{4,12},{5,1},{6,14},{7,3},{8,0},{9,13},{1... | collective-permute-start | bytes 196616 | tf_op jit(solution)/shard_map/ppermute | solution.py:240
  18.6 0.5 %collective-permute-done.5.other_ref = f32[16,1152]{1,0:T(8,128)S(1)} collective-permute-done((f32[16,1152]{1,0:T(8,128)S(1)}, f32[16,1152]{1,0:T(8,128)S(1)}, u32[]{:S(2)}, u32[]{:S(2)}) %collective-permute-start.5) | collective-permute-done | bytes 73760 | tf_op jit(solution)/shard_map/ppermute | solution.py:240
  19.1 0.7 %project.1 = (f32[8,1152]{1,0:T(8,128)S(1)}, f32[16,128]{1,0:T(8,128)S(1)}) custom-call(f32[16,1152]{1,0:T(8,128)S(1)} %add.15.mine_ref, f32[16,1152]{1,0:T(8,128)S(1)} %collective-permute-done.5.other_ref, bf16[1024,2048]{1,0:T(8,128)(2,1)S(1)} %get-tuple-element.15.acts_ref), custom_call_target="tpu_custom_call" | custom-call | tf_op jit(solution)/shard_map/project/pallas_call | solution.py:160
  19.7 1.6 %collective-permute-done.2.other_ref = f32[16,1024]{1,0:T(8,128)S(1)} collective-permute-done((f32[16,1024]{1,0:T(8,128)S(1)}, f32[16,1024]{1,0:T(8,128)S(1)}, u32[]{:S(2)}, u32[]{:S(2)}) %collective-permute-start.2) | collective-permute-done | bytes 65568 | tf_op jit(solution)/shard_map/ppermute | solution.py:240
  21.3 0.7 %project_rest.1 = (f32[2,1152]{1,0:T(2,128)S(1)}, f32[2,1152]{1,0:T(2,128)S(1)}, f32[2,1152]{1,0:T(2,128)S(1)}, f32[2,1152]{1,0:T(2,128)S(1)}) custom-call(f32[16,1024]{1,0:T(8,128)S(1)} %add.13.mine_ref, f32[16,1024]{1,0:T(8,128)S(1)} %collective-permute-done.2.other_ref, f32[16,128]{1,0:T(8,128)S(1)} %get-tuple-element.17.tally_ref, ...), custom_call_target="tpu_custom_call" | custom-call | tf_op jit(solution)/shard_map/project_rest/pallas_call | solution.py:199
  22.0 0.1 collective-permute-start.6
  22.1 1.6 %collective-permute-start.7 = (f32[2,1152]{1,0:T(2,128)S(1)}, f32[2,1152]{1,0:T(2,128)S(1)}, u32[]{:S(2)}, u32[]{:S(2)}) collective-permute-start(f32[2,1152]{1,0:T(2,128)S(1)} %get-tuple-element.21), channel_id=1, source_target_pairs={{0,2},{1,3},{2,0},{3,1},{4,6},{5,7},{6,4},{7,5},{8,10},{9,11},{10,... | collective-permute-start | bytes 27656 | tf_op jit(solution)/shard_map/ppermute | solution.py:244
  23.6 0.3 %collective-permute-start.8 = (f32[2,1152]{1,0:T(2,128)S(1)}, f32[2,1152]{1,0:T(2,128)S(1)}, u32[]{:S(2)}, u32[]{:S(2)}) collective-permute-start(f32[2,1152]{1,0:T(2,128)S(1)} %get-tuple-element.22), channel_id=1, source_target_pairs={{0,1},{1,0},{2,3},{3,2},{4,5},{5,4},{6,7},{7,6},{8,9},{9,8},{10,11... | collective-permute-start | bytes 27656 | tf_op jit(solution)/shard_map/ppermute | solution.py:244
  23.9 1.3 %collective-permute-done.6.refs_1_ = f32[2,1152]{1,0:T(2,128)S(1)} collective-permute-done((f32[2,1152]{1,0:T(2,128)S(1)}, f32[2,1152]{1,0:T(2,128)S(1)}, u32[]{:S(2)}, u32[]{:S(2)}) %collective-permute-start.6) | collective-permute-done | bytes 9248 | tf_op jit(solution)/shard_map/ppermute | solution.py:244
  25.2 0.6 %collective-permute-done.7.refs_2_ = f32[2,1152]{1,0:T(2,128)S(1)} collective-permute-done((f32[2,1152]{1,0:T(2,128)S(1)}, f32[2,1152]{1,0:T(2,128)S(1)}, u32[]{:S(2)}, u32[]{:S(2)}) %collective-permute-start.7) | collective-permute-done | bytes 9248 | tf_op jit(solution)/shard_map/ppermute | solution.py:244
  25.8 0.0 collective-permute-done.8.refs_3_
  25.8 0.7 %scale.1 = f32[2,1024]{1,0:T(2,128)} custom-call(f32[2,1152]{1,0:T(2,128)S(1)} %get-tuple-element.19.refs_0_, f32[2,1152]{1,0:T(2,128)S(1)} %collective-permute-done.6.refs_1_, f32[2,1152]{1,0:T(2,128)S(1)} %collective-permute-done.7.refs_2_, f32[2,1152]{1,0:T(2,128)S(1)} %collective-permute-done.8.refs_3_), custom_call_target="tpu_custom_call" | custom-call | tf_op jit(solution)/shard_map/scale/pallas_call | solution.py:221
  (4 shorter events, 0.0 us)
Async XLA Ops:
  3.2 5.4 %collective-permute-start.3 = (f32[16,1152]{1,0:T(8,128)S(1)}, f32[16,1152]{1,0:T(8,128)S(1)}, u32[]{:S(2)}, u32[]{:S(2)}) collective-permute-start(f32[16,1152]{1,0:T(8,128)S(1)} %get-tuple-element.16), channel_id=1, source_target_pairs={{0,4},{1,17},{2,6},{3,19},{4,0},{5,21},{6,2},{7,23},{8,12},{9,25},... | collective-permute-start | bytes 221192 | tf_op jit(solution)/shard_map/ppermute | solution.py:240
  6.6 5.1 %collective-permute-start = (f32[16,1024]{1,0:T(8,128)S(1)}, f32[16,1024]{1,0:T(8,128)S(1)}, u32[]{:S(2)}, u32[]{:S(2)}) collective-permute-start(f32[16,1024]{1,0:T(8,128)S(1)} %rest_sums.1), channel_id=1, source_target_pairs={{0,4},{1,17},{2,6},{3,19},{4,0},{5,21},{6,2},{7,23},{8,12},{9,25},... | collective-permute-start | bytes 196616 | tf_op jit(solution)/shard_map/ppermute | solution.py:240
  8.5 5.6 %collective-permute-start.4 = (f32[16,1152]{1,0:T(8,128)S(1)}, f32[16,1152]{1,0:T(8,128)S(1)}, u32[]{:S(2)}, u32[]{:S(2)}) collective-permute-start(f32[16,1152]{1,0:T(8,128)S(1)} %add.14), channel_id=1, source_target_pairs={{0,16},{1,9},{2,18},{3,11},{4,20},{5,13},{6,22},{7,15},{8,24},{9,1... | collective-permute-start | bytes 221192 | tf_op jit(solution)/shard_map/ppermute | solution.py:240
  11.7 5.2 %collective-permute-start.1 = (f32[16,1024]{1,0:T(8,128)S(1)}, f32[16,1024]{1,0:T(8,128)S(1)}, u32[]{:S(2)}, u32[]{:S(2)}) collective-permute-start(f32[16,1024]{1,0:T(8,128)S(1)} %add.12), channel_id=1, source_target_pairs={{0,16},{1,9},{2,18},{3,11},{4,20},{5,13},{6,22},{7,15},{8,24},{9,1... | collective-permute-start | bytes 196616 | tf_op jit(solution)/shard_map/ppermute | solution.py:240
  14.2 4.9 %collective-permute-start.5 = (f32[16,1152]{1,0:T(8,128)S(1)}, f32[16,1152]{1,0:T(8,128)S(1)}, u32[]{:S(2)}, u32[]{:S(2)}) collective-permute-start(f32[16,1152]{1,0:T(8,128)S(1)} %add.15.mine_ref), channel_id=1, source_target_pairs={{0,8},{1,5},{2,10},{3,7},{4,12},{5,1},{6,14},{7,3},{8,0},{9,13},{1... | collective-permute-start | bytes 221192 | tf_op jit(solution)/shard_map/ppermute | solution.py:240
  17.0 4.3 %collective-permute-start.2 = (f32[16,1024]{1,0:T(8,128)S(1)}, f32[16,1024]{1,0:T(8,128)S(1)}, u32[]{:S(2)}, u32[]{:S(2)}) collective-permute-start(f32[16,1024]{1,0:T(8,128)S(1)} %add.13.mine_ref), channel_id=1, source_target_pairs={{0,8},{1,5},{2,10},{3,7},{4,12},{5,1},{6,14},{7,3},{8,0},{9,13},{1... | collective-permute-start | bytes 196616 | tf_op jit(solution)/shard_map/ppermute | solution.py:240
  22.0 3.2 %collective-permute-start.6 = (f32[2,1152]{1,0:T(2,128)S(1)}, f32[2,1152]{1,0:T(2,128)S(1)}, u32[]{:S(2)}, u32[]{:S(2)}) collective-permute-start(f32[2,1152]{1,0:T(2,128)S(1)} %get-tuple-element.20), channel_id=1, source_target_pairs={{0,3},{1,2},{2,1},{3,0},{4,7},{5,6},{6,5},{7,4},{8,11},{9,10},{10,... | collective-permute-start | bytes 27656 | tf_op jit(solution)/shard_map/ppermute | solution.py:244
  22.1 3.7 %collective-permute-start.7 = (f32[2,1152]{1,0:T(2,128)S(1)}, f32[2,1152]{1,0:T(2,128)S(1)}, u32[]{:S(2)}, u32[]{:S(2)}) collective-permute-start(f32[2,1152]{1,0:T(2,128)S(1)} %get-tuple-element.21), channel_id=1, source_target_pairs={{0,2},{1,3},{2,0},{3,1},{4,6},{5,7},{6,4},{7,5},{8,10},{9,11},{10,... | collective-permute-start | bytes 27656 | tf_op jit(solution)/shard_map/ppermute | solution.py:244
  23.6 2.2 %collective-permute-start.8 = (f32[2,1152]{1,0:T(2,128)S(1)}, f32[2,1152]{1,0:T(2,128)S(1)}, u32[]{:S(2)}, u32[]{:S(2)}) collective-permute-start(f32[2,1152]{1,0:T(2,128)S(1)} %get-tuple-element.22), channel_id=1, source_target_pairs={{0,1},{1,0},{2,3},{3,2},{4,5},{5,4},{6,7},{7,6},{8,9},{9,8},{10,11... | collective-permute-start | bytes 27656 | tf_op jit(solution)/shard_map/ppermute | solution.py:244

commit v4 on v3

--- a/solution.py
+++ b/solution.py
@@ -1,5 +1,3 @@
-import functools
-
 import jax
 import jax.numpy as jnp
 from jax import lax
@@ -27,7 +25,7 @@
 
 
 def sums_kernel(
-    steps, counts_ref, cand_hbm, labels_hbm, acts_hbm, sums_ref, member_ref, acts_ref,
+    counts_ref, cand_hbm, labels_hbm, acts_hbm, sums_ref, member_ref, acts_ref,
     cand_ref, labels_ref, small_sems, sems,
 ):
     rows = acts_ref.shape[0]
@@ -35,7 +33,6 @@
     first = sums_ref.shape[1] - LANES
     cands = classes // 2
     prompts = labels_ref.shape[1]
-    tall = rows // steps
 
     small = [
         pltpu.make_async_copy(source, target, small_sems.at[place])
@@ -44,14 +41,16 @@
         )
     ]
 
-    def fetch(step):
-        part = pl.ds(step * tall, tall)
-        return pltpu.make_async_copy(acts_hbm.at[part, :], acts_ref.at[part, :], sems.at[step])
+    def fetch(part):
+        columns = (pl.ds(0, first), pl.ds(first, acts_ref.shape[1] - first))[part]
+        return pltpu.make_async_copy(
+            acts_hbm.at[:, columns], acts_ref.at[:, columns], sems.at[part]
+        )
 
     for copy in small:
         copy.start()
-    for step in range(steps):
-        fetch(step).start()
+    for part in range(2):
+        fetch(part).start()
 
     prompt_ids = lax.broadcasted_iota(jnp.int32, (prompts, rows), 0)
     prompt_of = lax.broadcasted_iota(jnp.int32, (prompts, rows), 1) // PER_PROMPT
@@ -70,23 +69,18 @@
     tally = jnp.sum(member_float, axis=1, keepdims=True)
     sums_ref[:, first:] = jnp.broadcast_to(tally, (classes, LANES))
 
-    total = None
-    for step in range(steps):
-        fetch(step).wait()
-        piece = jnp.dot(
-            member[:, step * tall : (step + 1) * tall],
-            acts_ref[step * tall : (step + 1) * tall, :first],
-            preferred_element_type=jnp.float32,
-        )
-        total = piece if total is None else total + piece
-    sums_ref[:, :first] = total
-
-
-def class_sums(activations, cand_index, labels, counts, classes, first, steps=8):
+    fetch(0).wait()
+    sums_ref[:, :first] = jnp.dot(
+        member, acts_ref[:, :first], preferred_element_type=jnp.float32
+    )
+    fetch(1).wait()
+
+
+def class_sums(activations, cand_index, labels, counts, classes, first):
     rows, width = activations.shape
     prompts = labels.shape[0]
     return pl.pallas_call(
-        functools.partial(sums_kernel, steps),
+        sums_kernel,
         out_shape=(
             jax.ShapeDtypeStruct((classes, first + LANES), jnp.float32),
             pltpu.VMEM((classes, rows), jnp.bfloat16),
@@ -98,7 +92,7 @@
             pltpu.VMEM((1, rows), jnp.int32),
             pltpu.VMEM((1, prompts), jnp.int32),
             pltpu.SemaphoreType.DMA((2,)),
-            pltpu.SemaphoreType.DMA((steps,)),
+            pltpu.SemaphoreType.DMA((2,)),
         ],
         compiler_params=pltpu.CompilerParams(vmem_limit_bytes=VMEM_LIMIT),
         name="class_sums",
@@ -228,14 +222,16 @@
     )(*shares)
 
 
-def dp_trade(value, step):
+def dp_trade(value, step, half):
     dp, feat = lax.axis_size("dp"), lax.axis_size("feat")
-    bits = [1 << b for b in range(dp.bit_length() - 1)]
-    bits = bits[:1] + bits[:0:-1]
+    count = dp.bit_length() - 1
+    up = list(range(count))
+    even = (up, up[:1] + up[:0:-1])[half]
+    odd = up[-1:] + up[:-1]
     pairs = []
     for d in range(dp):
         for f in range(feat):
-            bit = bits[(step + f % 2) % len(bits)]
+            bit = 1 << (odd if f % 2 else even)[step]
             pairs.append((d * feat + f, (d ^ bit) * feat + f))
     return lax.ppermute(value, ("dp", "feat"), pairs)
 
@@ -253,10 +249,10 @@
     rest = rest_sums(member, acts, first)
     rounds = dp.bit_length() - 1
     for step in range(rounds - 1):
-        sums = sums + dp_trade(sums, step)
-        rest = rest + dp_trade(rest, step)
-    shares, tally = project(sums, dp_trade(sums, rounds - 1), acts)
-    keep, *sends = project_rest(rest, dp_trade(rest, rounds - 1), tally, shares, acts)
+        sums = sums + dp_trade(sums, step, 0)
+        rest = rest + dp_trade(rest, step, 1)
+    shares, tally = project(sums, dp_trade(sums, rounds - 1, 0), acts)
+    keep, *sends = project_rest(rest, dp_trade(rest, rounds - 1, 1), tally, shares, acts)
     shares = [feat_trade(sends[bits - 1], bits) for bits in range(feat - 1, 0, -1)]
     return scale([keep] + shares).T
 

time: 26.6 us -> 25.6 us (0.962)
  waiting for transfers between devices: 6.67 us -> 6.05 us
    ppermute x6, waiting for transfers between devices: 4.78 us -> 4.17 us  [dp_trade(): return lax.ppermute(value, ('dp', 'feat'), pairs)]
  transfers between devices with their start and end apart: 9 -> 9, of which waited for: 7 -> 6; matrix products, arithmetic and copies ran while one was open for 0% -> 0% of each run, Pallas kernels for 4% -> 4%
where the time goes in v4:
time: 25.6 us; the launch traced here: 25.5 us
  starting transfers between devices  14 us (55%)
  waiting for transfers between devices  6.05 us (24%)
  Pallas kernels  4.68 us (18%)
  between operations  0.7 us (3%)
    ppermute x6, starting transfers between devices, dp_trade(): return lax.ppermute(value, ('dp', 'feat'), pairs)  12.1 us
    ppermute x6, waiting for transfers between devices, dp_trade(): return lax.ppermute(value, ('dp', 'feat'), pairs)  4.17 us
    pallas_call x1, Pallas kernels, class_sums(): pl.pallas_call(sums_kernel, out_shape=(jax.ShapeDtypeStruct((classes, fir...  2.29 us
    ppermute x3, starting transfers between devices, feat_trade(): lax.ppermute(value, 'feat', [(f, f ^ bits) for f in range(lax.axis_size('...  1.92 us
    ppermute x3, waiting for transfers between devices, feat_trade(): lax.ppermute(value, 'feat', [(f, f ^ bits) for f in range(lax.axis_size('...  1.88 us
    pallas_call x1, Pallas kernels, project_rest(): pl.pallas_call(project_rest_kernel, out_shape=(part,) * parts, in_specs=[...  0.68 us
    pallas_call x1, Pallas kernels, scale(): pl.pallas_call(scale_kernel, out_shape=jax.ShapeDtypeStruct((part, column...  0.68 us
    pallas_call x1, Pallas kernels, project(): pl.pallas_call(project_kernel, out_shape=(jax.ShapeDtypeStruct((classes /...  0.65 us
  transfers between devices with their start and end apart: 9, of which 6 were waited for; matrix products, arithmetic and copies ran while one was open for 0% of the time, Pallas kernels for 4%

profile of v4, /device:TPU:0, one launch (start us, length us, event | category | flops | bytes accessed | tf_op | source)
XLA Modules:
  0.0 25.5 jit_solution(618878641352548959)
XLA Ops:
  0.7 2.3 %class_sums.1 = (f32[16,1152]{1,0:T(8,128)S(1)}, bf16[16,1024]{1,0:T(8,128)(2,1)S(1)}, bf16[1024,2048]{1,0:T(8,128)(2,1)S(1)}) custom-call(s32[1]{0:T(128)S(6)} %copy.5.counts_ref, s32[1,1024]{1,0:T(1,128)} %bitcast.3, s32[1,64]{1,0:T(1,128)} %bitcast.4, bf16[1024,2048]{1,0:T(8,128)(2,1)} %acts_hbm.1), custom_call_target="tpu_custom_call" | custom-call | tf_op jit(solution)/shard_map/class_sums/pallas_call | solution.py:82
  2.9 3.0 %collective-permute-start.3 = (f32[16,1152]{1,0:T(8,128)S(1)}, f32[16,1152]{1,0:T(8,128)S(1)}, u32[]{:S(2)}, u32[]{:S(2)}) collective-permute-start(f32[16,1152]{1,0:T(8,128)S(1)} %get-tuple-element.16), channel_id=1, source_target_pairs={{0,4},{1,17},{2,6},{3,19},{4,0},{5,21},{6,2},{7,23},{8,12},{9,25},... | collective-permute-start | bytes 221192 | tf_op jit(solution)/shard_map/ppermute | solution.py:236
  6.0 0.4 %rest_sums.1 = f32[16,1024]{1,0:T(8,128)S(1)} custom-call(bf16[16,1024]{1,0:T(8,128)(2,1)S(1)} %get-tuple-element.14.member_ref, bf16[1024,2048]{1,0:T(8,128)(2,1)S(1)} %get-tuple-element.15.acts_ref), custom_call_target="tpu_custom_call" | custom-call | flops 33554432 | bytes 4194304 | tf_op jit(solution)/shard_map/rest_sums/pallas_call | solution.py:117
  6.4 0.0 collective-permute-start
  6.4 1.9 %collective-permute-done.3 = f32[16,1152]{1,0:T(8,128)S(1)} collective-permute-done((f32[16,1152]{1,0:T(8,128)S(1)}, f32[16,1152]{1,0:T(8,128)S(1)}, u32[]{:S(2)}, u32[]{:S(2)}) %collective-permute-start.3) | collective-permute-done | bytes 73760 | tf_op jit(solution)/shard_map/ppermute | solution.py:236
  8.3 2.1 %collective-permute-start.4 = (f32[16,1152]{1,0:T(8,128)S(1)}, f32[16,1152]{1,0:T(8,128)S(1)}, u32[]{:S(2)}, u32[]{:S(2)}) collective-permute-start(f32[16,1152]{1,0:T(8,128)S(1)} %add.14), channel_id=1, source_target_pairs={{0,8},{1,5},{2,10},{3,7},{4,12},{5,1},{6,14},{7,3},{8,0},{9,13},{1... | collective-permute-start | bytes 221192 | tf_op jit(solution)/shard_map/ppermute | solution.py:236
  10.5 0.2 collective-permute-done
  10.7 2.7 %collective-permute-start.1 = (f32[16,1024]{1,0:T(8,128)S(1)}, f32[16,1024]{1,0:T(8,128)S(1)}, u32[]{:S(2)}, u32[]{:S(2)}) collective-permute-start(f32[16,1024]{1,0:T(8,128)S(1)} %add.12), channel_id=1, source_target_pairs={{0,16},{1,5},{2,18},{3,7},{4,20},{5,1},{6,22},{7,3},{8,24},{9,13},... | collective-permute-start | bytes 196616 | tf_op jit(solution)/shard_map/ppermute | solution.py:236
  13.3 0.0 collective-permute-done.4
  13.3 2.6 %collective-permute-start.5 = (f32[16,1152]{1,0:T(8,128)S(1)}, f32[16,1152]{1,0:T(8,128)S(1)}, u32[]{:S(2)}, u32[]{:S(2)}) collective-permute-start(f32[16,1152]{1,0:T(8,128)S(1)} %add.15.mine_ref), channel_id=1, source_target_pairs={{0,16},{1,9},{2,18},{3,11},{4,20},{5,13},{6,22},{7,15},{8,24},{9,1... | collective-permute-start | bytes 221192 | tf_op jit(solution)/shard_map/ppermute | solution.py:236
  15.9 0.0 collective-permute-done.1
  15.9 1.6 %collective-permute-start.2 = (f32[16,1024]{1,0:T(8,128)S(1)}, f32[16,1024]{1,0:T(8,128)S(1)}, u32[]{:S(2)}, u32[]{:S(2)}) collective-permute-start(f32[16,1024]{1,0:T(8,128)S(1)} %add.13.mine_ref), channel_id=1, source_target_pairs={{0,8},{1,9},{2,10},{3,11},{4,12},{5,13},{6,14},{7,15},{8,0},{9,1},... | collective-permute-start | bytes 196616 | tf_op jit(solution)/shard_map/ppermute | solution.py:236
  17.6 1.1 %collective-permute-done.5.other_ref = f32[16,1152]{1,0:T(8,128)S(1)} collective-permute-done((f32[16,1152]{1,0:T(8,128)S(1)}, f32[16,1152]{1,0:T(8,128)S(1)}, u32[]{:S(2)}, u32[]{:S(2)}) %collective-permute-start.5) | collective-permute-done | bytes 73760 | tf_op jit(solution)/shard_map/ppermute | solution.py:236
  18.6 0.7 %project.1 = (f32[8,1152]{1,0:T(8,128)S(1)}, f32[16,128]{1,0:T(8,128)S(1)}) custom-call(f32[16,1152]{1,0:T(8,128)S(1)} %add.15.mine_ref, f32[16,1152]{1,0:T(8,128)S(1)} %collective-permute-done.5.other_ref, bf16[1024,2048]{1,0:T(8,128)(2,1)S(1)} %get-tuple-element.15.acts_ref), custom_call_target="tpu_custom_call" | custom-call | tf_op jit(solution)/shard_map/project/pallas_call | solution.py:154
  19.3 1.0 %collective-permute-done.2.other_ref = f32[16,1024]{1,0:T(8,128)S(1)} collective-permute-done((f32[16,1024]{1,0:T(8,128)S(1)}, f32[16,1024]{1,0:T(8,128)S(1)}, u32[]{:S(2)}, u32[]{:S(2)}) %collective-permute-start.2) | collective-permute-done | bytes 65568 | tf_op jit(solution)/shard_map/ppermute | solution.py:236
  20.3 0.7 %project_rest.1 = (f32[2,1152]{1,0:T(2,128)S(1)}, f32[2,1152]{1,0:T(2,128)S(1)}, f32[2,1152]{1,0:T(2,128)S(1)}, f32[2,1152]{1,0:T(2,128)S(1)}) custom-call(f32[16,1024]{1,0:T(8,128)S(1)} %add.13.mine_ref, f32[16,1024]{1,0:T(8,128)S(1)} %collective-permute-done.2.other_ref, f32[16,128]{1,0:T(8,128)S(1)} %get-tuple-element.17.tally_ref, ...), custom_call_target="tpu_custom_call" | custom-call | tf_op jit(solution)/shard_map/project_rest/pallas_call | solution.py:193
  21.0 0.1 collective-permute-start.6
  21.0 1.6 %collective-permute-start.7 = (f32[2,1152]{1,0:T(2,128)S(1)}, f32[2,1152]{1,0:T(2,128)S(1)}, u32[]{:S(2)}, u32[]{:S(2)}) collective-permute-start(f32[2,1152]{1,0:T(2,128)S(1)} %get-tuple-element.21), channel_id=1, source_target_pairs={{0,2},{1,3},{2,0},{3,1},{4,6},{5,7},{6,4},{7,5},{8,10},{9,11},{10,... | collective-permute-start | bytes 27656 | tf_op jit(solution)/shard_map/ppermute | solution.py:240
  22.6 0.3 %collective-permute-start.8 = (f32[2,1152]{1,0:T(2,128)S(1)}, f32[2,1152]{1,0:T(2,128)S(1)}, u32[]{:S(2)}, u32[]{:S(2)}) collective-permute-start(f32[2,1152]{1,0:T(2,128)S(1)} %get-tuple-element.22), channel_id=1, source_target_pairs={{0,1},{1,0},{2,3},{3,2},{4,5},{5,4},{6,7},{7,6},{8,9},{9,8},{10,11... | collective-permute-start | bytes 27656 | tf_op jit(solution)/shard_map/ppermute | solution.py:240
  22.9 1.3 %collective-permute-done.6.refs_1_ = f32[2,1152]{1,0:T(2,128)S(1)} collective-permute-done((f32[2,1152]{1,0:T(2,128)S(1)}, f32[2,1152]{1,0:T(2,128)S(1)}, u32[]{:S(2)}, u32[]{:S(2)}) %collective-permute-start.6) | collective-permute-done | bytes 9248 | tf_op jit(solution)/shard_map/ppermute | solution.py:240
  24.2 0.6 %collective-permute-done.7.refs_2_ = f32[2,1152]{1,0:T(2,128)S(1)} collective-permute-done((f32[2,1152]{1,0:T(2,128)S(1)}, f32[2,1152]{1,0:T(2,128)S(1)}, u32[]{:S(2)}, u32[]{:S(2)}) %collective-permute-start.7) | collective-permute-done | bytes 9248 | tf_op jit(solution)/shard_map/ppermute | solution.py:240
  24.8 0.0 collective-permute-done.8.refs_3_
  24.8 0.7 %scale.1 = f32[2,1024]{1,0:T(2,128)} custom-call(f32[2,1152]{1,0:T(2,128)S(1)} %get-tuple-element.19.refs_0_, f32[2,1152]{1,0:T(2,128)S(1)} %collective-permute-done.6.refs_1_, f32[2,1152]{1,0:T(2,128)S(1)} %collective-permute-done.7.refs_2_, f32[2,1152]{1,0:T(2,128)S(1)} %collective-permute-done.8.refs_3_), custom_call_target="tpu_custom_call" | custom-call | tf_op jit(solution)/shard_map/scale/pallas_call | solution.py:215
  (4 shorter events, 0.0 us)
Async XLA Ops:
  2.9 5.4 %collective-permute-start.3 = (f32[16,1152]{1,0:T(8,128)S(1)}, f32[16,1152]{1,0:T(8,128)S(1)}, u32[]{:S(2)}, u32[]{:S(2)}) collective-permute-start(f32[16,1152]{1,0:T(8,128)S(1)} %get-tuple-element.16), channel_id=1, source_target_pairs={{0,4},{1,17},{2,6},{3,19},{4,0},{5,21},{6,2},{7,23},{8,12},{9,25},... | collective-permute-start | bytes 221192 | tf_op jit(solution)/shard_map/ppermute | solution.py:236
  6.4 4.3 %collective-permute-start = (f32[16,1024]{1,0:T(8,128)S(1)}, f32[16,1024]{1,0:T(8,128)S(1)}, u32[]{:S(2)}, u32[]{:S(2)}) collective-permute-start(f32[16,1024]{1,0:T(8,128)S(1)} %rest_sums.1), channel_id=1, source_target_pairs={{0,4},{1,17},{2,6},{3,19},{4,0},{5,21},{6,2},{7,23},{8,12},{9,25},... | collective-permute-start | bytes 196616 | tf_op jit(solution)/shard_map/ppermute | solution.py:236
  8.3 5.0 %collective-permute-start.4 = (f32[16,1152]{1,0:T(8,128)S(1)}, f32[16,1152]{1,0:T(8,128)S(1)}, u32[]{:S(2)}, u32[]{:S(2)}) collective-permute-start(f32[16,1152]{1,0:T(8,128)S(1)} %add.14), channel_id=1, source_target_pairs={{0,8},{1,5},{2,10},{3,7},{4,12},{5,1},{6,14},{7,3},{8,0},{9,13},{1... | collective-permute-start | bytes 221192 | tf_op jit(solution)/shard_map/ppermute | solution.py:236
  10.7 5.3 %collective-permute-start.1 = (f32[16,1024]{1,0:T(8,128)S(1)}, f32[16,1024]{1,0:T(8,128)S(1)}, u32[]{:S(2)}, u32[]{:S(2)}) collective-permute-start(f32[16,1024]{1,0:T(8,128)S(1)} %add.12), channel_id=1, source_target_pairs={{0,16},{1,5},{2,18},{3,7},{4,20},{5,1},{6,22},{7,3},{8,24},{9,13},... | collective-permute-start | bytes 196616 | tf_op jit(solution)/shard_map/ppermute | solution.py:236
  13.3 5.3 %collective-permute-start.5 = (f32[16,1152]{1,0:T(8,128)S(1)}, f32[16,1152]{1,0:T(8,128)S(1)}, u32[]{:S(2)}, u32[]{:S(2)}) collective-permute-start(f32[16,1152]{1,0:T(8,128)S(1)} %add.15.mine_ref), channel_id=1, source_target_pairs={{0,16},{1,9},{2,18},{3,11},{4,20},{5,13},{6,22},{7,15},{8,24},{9,1... | collective-permute-start | bytes 221192 | tf_op jit(solution)/shard_map/ppermute | solution.py:236
  15.9 4.3 %collective-permute-start.2 = (f32[16,1024]{1,0:T(8,128)S(1)}, f32[16,1024]{1,0:T(8,128)S(1)}, u32[]{:S(2)}, u32[]{:S(2)}) collective-permute-start(f32[16,1024]{1,0:T(8,128)S(1)} %add.13.mine_ref), channel_id=1, source_target_pairs={{0,8},{1,9},{2,10},{3,11},{4,12},{5,13},{6,14},{7,15},{8,0},{9,1},... | collective-permute-start | bytes 196616 | tf_op jit(solution)/shard_map/ppermute | solution.py:236
  21.0 3.2 %collective-permute-start.6 = (f32[2,1152]{1,0:T(2,128)S(1)}, f32[2,1152]{1,0:T(2,128)S(1)}, u32[]{:S(2)}, u32[]{:S(2)}) collective-permute-start(f32[2,1152]{1,0:T(2,128)S(1)} %get-tuple-element.20), channel_id=1, source_target_pairs={{0,3},{1,2},{2,1},{3,0},{4,7},{5,6},{6,5},{7,4},{8,11},{9,10},{10,... | collective-permute-start | bytes 27656 | tf_op jit(solution)/shard_map/ppermute | solution.py:240
  21.0 3.7 %collective-permute-start.7 = (f32[2,1152]{1,0:T(2,128)S(1)}, f32[2,1152]{1,0:T(2,128)S(1)}, u32[]{:S(2)}, u32[]{:S(2)}) collective-permute-start(f32[2,1152]{1,0:T(2,128)S(1)} %get-tuple-element.21), channel_id=1, source_target_pairs={{0,2},{1,3},{2,0},{3,1},{4,6},{5,7},{6,4},{7,5},{8,10},{9,11},{10,... | collective-permute-start | bytes 27656 | tf_op jit(solution)/shard_map/ppermute | solution.py:240
  22.6 2.2 %collective-permute-start.8 = (f32[2,1152]{1,0:T(2,128)S(1)}, f32[2,1152]{1,0:T(2,128)S(1)}, u32[]{:S(2)}, u32[]{:S(2)}) collective-permute-start(f32[2,1152]{1,0:T(2,128)S(1)} %get-tuple-element.22), channel_id=1, source_target_pairs={{0,1},{1,0},{2,3},{3,2},{4,5},{5,4},{6,7},{7,6},{8,9},{9,8},{10,11... | collective-permute-start | bytes 27656 | tf_op jit(solution)/shard_map/ppermute | solution.py:240

commit v5 on v4

--- a/solution.py
+++ b/solution.py
@@ -24,84 +24,73 @@
     return pltpu.with_memory_space_constraint(value, pltpu.VMEM)
 
 
-def sums_kernel(
-    counts_ref, cand_hbm, labels_hbm, acts_hbm, sums_ref, member_ref, acts_ref,
-    cand_ref, labels_ref, small_sems, sems,
-):
-    rows = acts_ref.shape[0]
-    classes = sums_ref.shape[0]
-    first = sums_ref.shape[1] - LANES
+def member_kernel(counts_ref, cand_hbm, labels_hbm, member_ref, tally_ref, cand_ref, labels_ref, sems):
+    classes, rows = member_ref.shape
     cands = classes // 2
     prompts = labels_ref.shape[1]
-
-    small = [
-        pltpu.make_async_copy(source, target, small_sems.at[place])
+    copies = [
+        pltpu.make_async_copy(source, target, sems.at[place])
         for place, (source, target) in enumerate(
             ((cand_hbm, cand_ref), (labels_hbm, labels_ref))
         )
     ]
-
-    def fetch(part):
-        columns = (pl.ds(0, first), pl.ds(first, acts_ref.shape[1] - first))[part]
-        return pltpu.make_async_copy(
-            acts_hbm.at[:, columns], acts_ref.at[:, columns], sems.at[part]
-        )
-
-    for copy in small:
+    for copy in copies:
         copy.start()
-    for part in range(2):
-        fetch(part).start()
-
     prompt_ids = lax.broadcasted_iota(jnp.int32, (prompts, rows), 0)
     prompt_of = lax.broadcasted_iota(jnp.int32, (prompts, rows), 1) // PER_PROMPT
     spread = jnp.where(prompt_ids == prompt_of, 1.0, 0.0).astype(jnp.bfloat16)
     wanted = lax.broadcasted_iota(jnp.int32, (classes, rows), 0)
     row_prompt = lax.broadcasted_iota(jnp.int32, (1, rows), 1) // PER_PROMPT
-    for copy in small:
+    for copy in copies:
         copy.wait()
     labels = jnp.broadcast_to(labels_ref[...].astype(jnp.float32), (8, prompts))
     row_class = jnp.dot(labels.astype(jnp.bfloat16), spread, preferred_element_type=jnp.float32)[:1]
     slot = jnp.where(row_class == 1.0, cand_ref[...], cand_ref[...] + cands)
     slot = jnp.where(row_prompt < counts_ref[0], slot, -1)
-    member_float = jnp.where(wanted == slot, 1.0, 0.0)
-    member = member_float.astype(jnp.bfloat16)
-    member_ref[...] = member
-    tally = jnp.sum(member_float, axis=1, keepdims=True)
-    sums_ref[:, first:] = jnp.broadcast_to(tally, (classes, LANES))
-
-    fetch(0).wait()
-    sums_ref[:, :first] = jnp.dot(
-        member, acts_ref[:, :first], preferred_element_type=jnp.float32
-    )
-    fetch(1).wait()
-
-
-def class_sums(activations, cand_index, labels, counts, classes, first):
-    rows, width = activations.shape
-    prompts = labels.shape[0]
-    return pl.pallas_call(
-        sums_kernel,
+    member = jnp.where(wanted == slot, 1.0, 0.0)
+    member_ref[...] = member.astype(jnp.bfloat16)
+    tally = jnp.sum(member, axis=1, keepdims=True)
+    tally_ref[...] = jnp.broadcast_to(tally, (classes, LANES))
+
+
+def membership(cand_index, labels, counts, classes, width):
+    rows, prompts = cand_index.shape[0], labels.shape[0]
+    return pl.pallas_call(
+        member_kernel,
         out_shape=(
-            jax.ShapeDtypeStruct((classes, first + LANES), jnp.float32),
-            pltpu.VMEM((classes, rows), jnp.bfloat16),
-            pltpu.VMEM((rows, width), activations.dtype),
+            jax.ShapeDtypeStruct((classes, rows), jnp.bfloat16),
+            jax.ShapeDtypeStruct((classes, LANES), jnp.float32),
         ),
-        in_specs=[pl.BlockSpec(memory_space=pltpu.SMEM)] + [HBM] * 3,
-        out_specs=(VMEM,) * 3,
+        in_specs=[pl.BlockSpec(memory_space=pltpu.SMEM)] + [HBM] * 2,
+        out_specs=(VMEM,) * 2,
         scratch_shapes=[
             pltpu.VMEM((1, rows), jnp.int32),
             pltpu.VMEM((1, prompts), jnp.int32),
             pltpu.SemaphoreType.DMA((2,)),
-            pltpu.SemaphoreType.DMA((2,)),
         ],
-        compiler_params=pltpu.CompilerParams(vmem_limit_bytes=VMEM_LIMIT),
-        name="class_sums",
-    )(
-        counts,
-        in_hbm(cand_index.reshape(1, rows)),
-        in_hbm(labels.reshape(1, prompts)),
-        in_hbm(activations),
-    )
+        cost_estimate=pl.CostEstimate(flops=800 * rows * width, bytes_accessed=0, transcendentals=0),
+        compiler_params=pltpu.CompilerParams(vmem_limit_bytes=VMEM_LIMIT),
+        name="membership",
+    )(counts, in_hbm(cand_index.reshape(1, rows)), in_hbm(labels.reshape(1, prompts)))
+
+
+def first_kernel(member_ref, tally_ref, acts_ref, sums_ref):
+    first = sums_ref.shape[1] - LANES
+    sums_ref[:, :first] = jnp.dot(
+        member_ref[...], acts_ref[:, :first], preferred_element_type=jnp.float32
+    )
+    sums_ref[:, first:] = tally_ref[...]
+
+
+def first_sums(member, tally, acts, first):
+    return pl.pallas_call(
+        first_kernel,
+        out_shape=jax.ShapeDtypeStruct((member.shape[0], first + LANES), jnp.float32),
+        in_specs=[VMEM] * 3,
+        out_specs=VMEM,
+        compiler_params=pltpu.CompilerParams(vmem_limit_bytes=VMEM_LIMIT),
+        name="first_sums",
+    )(in_vmem(member), in_vmem(tally), acts)
 
 
 def rest_kernel(member_ref, acts_ref, sums_ref):
@@ -112,19 +101,14 @@
 
 
 def rest_sums(member, acts, first):
-    rows, width = acts.shape
-    classes = member.shape[0]
     return pl.pallas_call(
         rest_kernel,
-        out_shape=jax.ShapeDtypeStruct((classes, width - first), jnp.float32),
+        out_shape=jax.ShapeDtypeStruct((member.shape[0], acts.shape[1] - first), jnp.float32),
         in_specs=[VMEM] * 2,
         out_specs=VMEM,
-        cost_estimate=pl.CostEstimate(
-            flops=2 * classes * rows * (width - first), bytes_accessed=2 * rows * width, transcendentals=0
-        ),
         compiler_params=pltpu.CompilerParams(vmem_limit_bytes=VMEM_LIMIT),
         name="rest_sums",
-    )(in_vmem(member), in_vmem(acts))
+    )(in_vmem(member), acts)
 
 
 def directions(total, tally):
@@ -161,19 +145,18 @@
         out_specs=(VMEM,) * 2,
         compiler_params=pltpu.CompilerParams(vmem_limit_bytes=VMEM_LIMIT),
         name="project",
-    )(mine, other, in_vmem(acts))
+    )(mine, other, acts)
 
 
 def project_rest_kernel(mine_ref, other_ref, tally_ref, shares_ref, acts_ref, keep_ref, *send_refs):
-    rows, width = acts_ref.shape
-    first = width - mine_ref.shape[1]
+    rows = acts_ref.shape[0]
     cands = mine_ref.shape[0] // 2
     parts = len(send_refs) + 1
     part = cands // parts
     place = lax.axis_index("feat")
     raw_dir, squares = directions(mine_ref[...] + other_ref[...], tally_ref[:, :1])
     plain = lax.dot_general(
-        raw_dir, acts_ref[:, first:], (((1,), (1,)), ((), ())), preferred_element_type=jnp.float32
+        raw_dir, acts_ref[:, acts_ref.shape[1] - mine_ref.shape[1]:], (((1,), (1,)), ((), ())), preferred_element_type=jnp.float32
     )
     plain = plain + shares_ref[:, :rows]
     squares = squares + shares_ref[:, rows:]
@@ -197,7 +180,7 @@
         out_specs=(VMEM,) * parts,
         compiler_params=pltpu.CompilerParams(vmem_limit_bytes=VMEM_LIMIT),
         name="project_rest",
-    )(mine, other, tally, shares, in_vmem(acts))
+    )(mine, other, tally, shares, acts)
 
 
 def scale_kernel(*refs):
@@ -243,9 +226,10 @@
 def per_device(activations, cand_index, labels, counts):
     dp, feat = lax.axis_size("dp"), lax.axis_size("feat")
     first = activations.shape[1] // 2
-    sums, member, acts = class_sums(
-        activations, cand_index, labels, counts, 2 * CAND_DEV * dp, first
-    )
+    classes = 2 * CAND_DEV * dp
+    acts = in_vmem(activations)
+    member, tally = membership(cand_index, labels, counts, classes, activations.shape[1])
+    sums = first_sums(member, tally, acts, first)
     rest = rest_sums(member, acts, first)
     rounds = dp.bit_length() - 1
     for step in range(rounds - 1):

time: 25.6 us -> 25.3 us (0.988)
  Pallas kernels: 4.68 us -> 3.85 us
  local copies, waits for them, and re-layouts: 0 us -> 0.34 us
    pallas_call x2 -> x3, Pallas kernels: 2.66 us -> 1.83 us  [the longest x1 1.08 us: membership(): pl.pallas_call(member_kernel, out_shape=(jax.ShapeDtypeStruct((classes, r...]
    unnamed x0 -> x2, local copies, waits for them, and re-layouts: none -> 0.34 us
where the time goes in v5:
time: 25.3 us; the launch traced here: 25.1 us
  starting transfers between devices  13.9 us (55%)
  waiting for transfers between devices  6.06 us (24%)
  Pallas kernels  3.85 us (15%)
  between operations  0.85 us (3%)
  local copies, waits for them, and re-layouts  0.34 us (1%)
    ppermute x6, starting transfers between devices, dp_trade(): return lax.ppermute(value, ('dp', 'feat'), pairs)  12 us
    ppermute x6, waiting for transfers between devices, dp_trade(): return lax.ppermute(value, ('dp', 'feat'), pairs)  4.17 us
    ppermute x3, starting transfers between devices, feat_trade(): lax.ppermute(value, 'feat', [(f, f ^ bits) for f in range(lax.axis_size('...  1.92 us
    ppermute x3, waiting for transfers between devices, feat_trade(): lax.ppermute(value, 'feat', [(f, f ^ bits) for f in range(lax.axis_size('...  1.88 us
    pallas_call x1, Pallas kernels, membership(): pl.pallas_call(member_kernel, out_shape=(jax.ShapeDtypeStruct((classes, r...  1.08 us
    pallas_call x1, Pallas kernels, project_rest(): pl.pallas_call(project_rest_kernel, out_shape=(part,) * parts, in_specs=[...  0.68 us
    pallas_call x1, Pallas kernels, scale(): pl.pallas_call(scale_kernel, out_shape=jax.ShapeDtypeStruct((part, column...  0.68 us
    pallas_call x1, Pallas kernels, project(): pl.pallas_call(project_kernel, out_shape=(jax.ShapeDtypeStruct((classes /...  0.65 us
  transfers between devices with their start and end apart: 9, of which 6 were waited for; matrix products, arithmetic and copies ran while one was open for 0% of the time, Pallas kernels for 4%

profile of v5, /device:TPU:0, one launch (start us, length us, event | category | flops | bytes accessed | tf_op | source)
XLA Modules:
  0.0 25.1 jit_solution(10897836262257944830)
XLA Ops:
  0.8 1.1 %membership.1 = (bf16[16,1024]{1,0:T(8,128)(2,1)S(1)}, f32[16,128]{1,0:T(8,128)S(1)}) custom-call(s32[1]{0:T(128)S(6)} %copy.5.counts_ref, s32[1,1024]{1,0:T(1,128)} %bitcast.3, s32[1,64]{1,0:T(1,128)} %bitcast.4), custom_call_target="tpu_custom_call" | custom-call | flops 1677721600 | tf_op jit(solution)/shard_map/membership/pallas_call | solution.py:58
  1.9 0.3 %copy-done = bf16[1024,2048]{1,0:T(8,128)(2,1)S(1)} copy-done((bf16[1024,2048]{1,0:T(8,128)(2,1)S(1)}, bf16[1024,2048]{1,0:T(8,128)(2,1)}, u32[]{:S(2)}) %copy-start) | copy-done | bytes 4194328
  2.2 0.4 %first_sums.1 = f32[16,1152]{1,0:T(8,128)S(1)} custom-call(bf16[16,1024]{1,0:T(8,128)(2,1)S(1)} %get-tuple-element.13.member_ref, f32[16,128]{1,0:T(8,128)S(1)} %get-tuple-element.14.tally_ref, bf16[1024,2048]{1,0:T(8,128)(2,1)S(1)} %copy-done), custom_call_target="tpu_custom_call" | custom-call | tf_op jit(solution)/shard_map/first_sums/pallas_call | solution.py:86
  2.6 3.0 %collective-permute-start.3 = (f32[16,1152]{1,0:T(8,128)S(1)}, f32[16,1152]{1,0:T(8,128)S(1)}, u32[]{:S(2)}, u32[]{:S(2)}) collective-permute-start(f32[16,1152]{1,0:T(8,128)S(1)} %first_sums.1), channel_id=1, source_target_pairs={{0,4},{1,17},{2,6},{3,19},{4,0},{5,21},{6,2},{7,23},{8,12},{9,25},... | collective-permute-start | bytes 221192 | tf_op jit(solution)/shard_map/ppermute | solution.py:219
  5.6 0.4 %rest_sums.1 = f32[16,1024]{1,0:T(8,128)S(1)} custom-call(bf16[16,1024]{1,0:T(8,128)(2,1)S(1)} %get-tuple-element.13.member_ref, bf16[1024,2048]{1,0:T(8,128)(2,1)S(1)} %copy-done), custom_call_target="tpu_custom_call" | custom-call | tf_op jit(solution)/shard_map/rest_sums/pallas_call | solution.py:104
  6.0 0.0 collective-permute-start
  6.0 1.9 %collective-permute-done.3 = f32[16,1152]{1,0:T(8,128)S(1)} collective-permute-done((f32[16,1152]{1,0:T(8,128)S(1)}, f32[16,1152]{1,0:T(8,128)S(1)}, u32[]{:S(2)}, u32[]{:S(2)}) %collective-permute-start.3) | collective-permute-done | bytes 73760 | tf_op jit(solution)/shard_map/ppermute | solution.py:219
  7.9 2.1 %collective-permute-start.4 = (f32[16,1152]{1,0:T(8,128)S(1)}, f32[16,1152]{1,0:T(8,128)S(1)}, u32[]{:S(2)}, u32[]{:S(2)}) collective-permute-start(f32[16,1152]{1,0:T(8,128)S(1)} %add.14), channel_id=1, source_target_pairs={{0,8},{1,5},{2,10},{3,7},{4,12},{5,1},{6,14},{7,3},{8,0},{9,13},{1... | collective-permute-start | bytes 221192 | tf_op jit(solution)/shard_map/ppermute | solution.py:219
  10.1 0.2 collective-permute-done
  10.3 2.7 %collective-permute-start.1 = (f32[16,1024]{1,0:T(8,128)S(1)}, f32[16,1024]{1,0:T(8,128)S(1)}, u32[]{:S(2)}, u32[]{:S(2)}) collective-permute-start(f32[16,1024]{1,0:T(8,128)S(1)} %add.12), channel_id=1, source_target_pairs={{0,16},{1,5},{2,18},{3,7},{4,20},{5,1},{6,22},{7,3},{8,24},{9,13},... | collective-permute-start | bytes 196616 | tf_op jit(solution)/shard_map/ppermute | solution.py:219
  12.9 0.0 collective-permute-done.4
  12.9 2.6 %collective-permute-start.5 = (f32[16,1152]{1,0:T(8,128)S(1)}, f32[16,1152]{1,0:T(8,128)S(1)}, u32[]{:S(2)}, u32[]{:S(2)}) collective-permute-start(f32[16,1152]{1,0:T(8,128)S(1)} %add.15.mine_ref), channel_id=1, source_target_pairs={{0,16},{1,9},{2,18},{3,11},{4,20},{5,13},{6,22},{7,15},{8,24},{9,1... | collective-permute-start | bytes 221192 | tf_op jit(solution)/shard_map/ppermute | solution.py:219
  15.5 0.0 collective-permute-done.1
  15.6 1.6 %collective-permute-start.2 = (f32[16,1024]{1,0:T(8,128)S(1)}, f32[16,1024]{1,0:T(8,128)S(1)}, u32[]{:S(2)}, u32[]{:S(2)}) collective-permute-start(f32[16,1024]{1,0:T(8,128)S(1)} %add.13.mine_ref), channel_id=1, source_target_pairs={{0,8},{1,9},{2,10},{3,11},{4,12},{5,13},{6,14},{7,15},{8,0},{9,1},... | collective-permute-start | bytes 196616 | tf_op jit(solution)/shard_map/ppermute | solution.py:219
  17.2 1.1 %collective-permute-done.5.other_ref = f32[16,1152]{1,0:T(8,128)S(1)} collective-permute-done((f32[16,1152]{1,0:T(8,128)S(1)}, f32[16,1152]{1,0:T(8,128)S(1)}, u32[]{:S(2)}, u32[]{:S(2)}) %collective-permute-start.5) | collective-permute-done | bytes 73760 | tf_op jit(solution)/shard_map/ppermute | solution.py:219
  18.3 0.7 %project.1 = (f32[8,1152]{1,0:T(8,128)S(1)}, f32[16,128]{1,0:T(8,128)S(1)}) custom-call(f32[16,1152]{1,0:T(8,128)S(1)} %add.15.mine_ref, f32[16,1152]{1,0:T(8,128)S(1)} %collective-permute-done.5.other_ref, bf16[1024,2048]{1,0:T(8,128)(2,1)S(1)} %copy-done), custom_call_target="tpu_custom_call" | custom-call | tf_op jit(solution)/shard_map/project/pallas_call | solution.py:138
  18.9 1.0 %collective-permute-done.2.other_ref = f32[16,1024]{1,0:T(8,128)S(1)} collective-permute-done((f32[16,1024]{1,0:T(8,128)S(1)}, f32[16,1024]{1,0:T(8,128)S(1)}, u32[]{:S(2)}, u32[]{:S(2)}) %collective-permute-start.2) | collective-permute-done | bytes 65568 | tf_op jit(solution)/shard_map/ppermute | solution.py:219
  19.9 0.7 %project_rest.1 = (f32[2,1152]{1,0:T(2,128)S(1)}, f32[2,1152]{1,0:T(2,128)S(1)}, f32[2,1152]{1,0:T(2,128)S(1)}, f32[2,1152]{1,0:T(2,128)S(1)}) custom-call(f32[16,1024]{1,0:T(8,128)S(1)} %add.13.mine_ref, f32[16,1024]{1,0:T(8,128)S(1)} %collective-permute-done.2.other_ref, f32[16,128]{1,0:T(8,128)S(1)} %get-tuple-element.15.tally_ref, ...), custom_call_target="tpu_custom_call" | custom-call | tf_op jit(solution)/shard_map/project_rest/pallas_call | solution.py:176
  20.6 0.1 collective-permute-start.6
  20.7 1.6 %collective-permute-start.7 = (f32[2,1152]{1,0:T(2,128)S(1)}, f32[2,1152]{1,0:T(2,128)S(1)}, u32[]{:S(2)}, u32[]{:S(2)}) collective-permute-start(f32[2,1152]{1,0:T(2,128)S(1)} %get-tuple-element.19), channel_id=1, source_target_pairs={{0,2},{1,3},{2,0},{3,1},{4,6},{5,7},{6,4},{7,5},{8,10},{9,11},{10,... | collective-permute-start | bytes 27656 | tf_op jit(solution)/shard_map/ppermute | solution.py:223
  22.2 0.3 %collective-permute-start.8 = (f32[2,1152]{1,0:T(2,128)S(1)}, f32[2,1152]{1,0:T(2,128)S(1)}, u32[]{:S(2)}, u32[]{:S(2)}) collective-permute-start(f32[2,1152]{1,0:T(2,128)S(1)} %get-tuple-element.20), channel_id=1, source_target_pairs={{0,1},{1,0},{2,3},{3,2},{4,5},{5,4},{6,7},{7,6},{8,9},{9,8},{10,11... | collective-permute-start | bytes 27656 | tf_op jit(solution)/shard_map/ppermute | solution.py:223
  22.5 1.3 %collective-permute-done.6.refs_1_ = f32[2,1152]{1,0:T(2,128)S(1)} collective-permute-done((f32[2,1152]{1,0:T(2,128)S(1)}, f32[2,1152]{1,0:T(2,128)S(1)}, u32[]{:S(2)}, u32[]{:S(2)}) %collective-permute-start.6) | collective-permute-done | bytes 9248 | tf_op jit(solution)/shard_map/ppermute | solution.py:223
  23.8 0.6 %collective-permute-done.7.refs_2_ = f32[2,1152]{1,0:T(2,128)S(1)} collective-permute-done((f32[2,1152]{1,0:T(2,128)S(1)}, f32[2,1152]{1,0:T(2,128)S(1)}, u32[]{:S(2)}, u32[]{:S(2)}) %collective-permute-start.7) | collective-permute-done | bytes 9248 | tf_op jit(solution)/shard_map/ppermute | solution.py:223
  24.4 0.7 %scale.1 = f32[2,1024]{1,0:T(2,128)} custom-call(f32[2,1152]{1,0:T(2,128)S(1)} %get-tuple-element.17.refs_0_, f32[2,1152]{1,0:T(2,128)S(1)} %collective-permute-done.6.refs_1_, f32[2,1152]{1,0:T(2,128)S(1)} %collective-permute-done.7.refs_2_, f32[2,1152]{1,0:T(2,128)S(1)} %collective-permute-done.8.refs_3_), custom_call_target="tpu_custom_call" | custom-call | tf_op jit(solution)/shard_map/scale/pallas_call | solution.py:198
  (6 shorter events, 0.0 us)
Async XLA Ops:
  0.0 2.2 %copy-start = (bf16[1024,2048]{1,0:T(8,128)(2,1)S(1)}, bf16[1024,2048]{1,0:T(8,128)(2,1)}, u32[]{:S(2)}) copy-start(bf16[1024,2048]{1,0:T(8,128)(2,1)} %acts_ref.7) | copy-start | bytes 12582916
  2.6 5.3 %collective-permute-start.3 = (f32[16,1152]{1,0:T(8,128)S(1)}, f32[16,1152]{1,0:T(8,128)S(1)}, u32[]{:S(2)}, u32[]{:S(2)}) collective-permute-start(f32[16,1152]{1,0:T(8,128)S(1)} %first_sums.1), channel_id=1, source_target_pairs={{0,4},{1,17},{2,6},{3,19},{4,0},{5,21},{6,2},{7,23},{8,12},{9,25},... | collective-permute-start | bytes 221192 | tf_op jit(solution)/shard_map/ppermute | solution.py:219
  6.0 4.3 %collective-permute-start = (f32[16,1024]{1,0:T(8,128)S(1)}, f32[16,1024]{1,0:T(8,128)S(1)}, u32[]{:S(2)}, u32[]{:S(2)}) collective-permute-start(f32[16,1024]{1,0:T(8,128)S(1)} %rest_sums.1), channel_id=1, source_target_pairs={{0,4},{1,17},{2,6},{3,19},{4,0},{5,21},{6,2},{7,23},{8,12},{9,25},... | collective-permute-start | bytes 196616 | tf_op jit(solution)/shard_map/ppermute | solution.py:219
  7.9 5.0 %collective-permute-start.4 = (f32[16,1152]{1,0:T(8,128)S(1)}, f32[16,1152]{1,0:T(8,128)S(1)}, u32[]{:S(2)}, u32[]{:S(2)}) collective-permute-start(f32[16,1152]{1,0:T(8,128)S(1)} %add.14), channel_id=1, source_target_pairs={{0,8},{1,5},{2,10},{3,7},{4,12},{5,1},{6,14},{7,3},{8,0},{9,13},{1... | collective-permute-start | bytes 221192 | tf_op jit(solution)/shard_map/ppermute | solution.py:219
  10.3 5.3 %collective-permute-start.1 = (f32[16,1024]{1,0:T(8,128)S(1)}, f32[16,1024]{1,0:T(8,128)S(1)}, u32[]{:S(2)}, u32[]{:S(2)}) collective-permute-start(f32[16,1024]{1,0:T(8,128)S(1)} %add.12), channel_id=1, source_target_pairs={{0,16},{1,5},{2,18},{3,7},{4,20},{5,1},{6,22},{7,3},{8,24},{9,13},... | collective-permute-start | bytes 196616 | tf_op jit(solution)/shard_map/ppermute | solution.py:219
  12.9 5.3 %collective-permute-start.5 = (f32[16,1152]{1,0:T(8,128)S(1)}, f32[16,1152]{1,0:T(8,128)S(1)}, u32[]{:S(2)}, u32[]{:S(2)}) collective-permute-start(f32[16,1152]{1,0:T(8,128)S(1)} %add.15.mine_ref), channel_id=1, source_target_pairs={{0,16},{1,9},{2,18},{3,11},{4,20},{5,13},{6,22},{7,15},{8,24},{9,1... | collective-permute-start | bytes 221192 | tf_op jit(solution)/shard_map/ppermute | solution.py:219
  15.6 4.3 %collective-permute-start.2 = (f32[16,1024]{1,0:T(8,128)S(1)}, f32[16,1024]{1,0:T(8,128)S(1)}, u32[]{:S(2)}, u32[]{:S(2)}) collective-permute-start(f32[16,1024]{1,0:T(8,128)S(1)} %add.13.mine_ref), channel_id=1, source_target_pairs={{0,8},{1,9},{2,10},{3,11},{4,12},{5,13},{6,14},{7,15},{8,0},{9,1},... | collective-permute-start | bytes 196616 | tf_op jit(solution)/shard_map/ppermute | solution.py:219
  20.6 3.2 %collective-permute-start.6 = (f32[2,1152]{1,0:T(2,128)S(1)}, f32[2,1152]{1,0:T(2,128)S(1)}, u32[]{:S(2)}, u32[]{:S(2)}) collective-permute-start(f32[2,1152]{1,0:T(2,128)S(1)} %get-tuple-element.18), channel_id=1, source_target_pairs={{0,3},{1,2},{2,1},{3,0},{4,7},{5,6},{6,5},{7,4},{8,11},{9,10},{10,... | collective-permute-start | bytes 27656 | tf_op jit(solution)/shard_map/ppermute | solution.py:223
  20.7 3.7 %collective-permute-start.7 = (f32[2,1152]{1,0:T(2,128)S(1)}, f32[2,1152]{1,0:T(2,128)S(1)}, u32[]{:S(2)}, u32[]{:S(2)}) collective-permute-start(f32[2,1152]{1,0:T(2,128)S(1)} %get-tuple-element.19), channel_id=1, source_target_pairs={{0,2},{1,3},{2,0},{3,1},{4,6},{5,7},{6,4},{7,5},{8,10},{9,11},{10,... | collective-permute-start | bytes 27656 | tf_op jit(solution)/shard_map/ppermute | solution.py:223
  22.2 2.2 %collective-permute-start.8 = (f32[2,1152]{1,0:T(2,128)S(1)}, f32[2,1152]{1,0:T(2,128)S(1)}, u32[]{:S(2)}, u32[]{:S(2)}) collective-permute-start(f32[2,1152]{1,0:T(2,128)S(1)} %get-tuple-element.20), channel_id=1, source_target_pairs={{0,1},{1,0},{2,3},{3,2},{4,5},{5,4},{6,7},{7,6},{8,9},{9,8},{10,11... | collective-permute-start | bytes 27656 | tf_op jit(solution)/shard_map/ppermute | solution.py:223

commit v6 on v5

--- a/solution.py
+++ b/solution.py
@@ -148,16 +148,31 @@
     )(mine, other, acts)
 
 
-def project_rest_kernel(mine_ref, other_ref, tally_ref, shares_ref, acts_ref, keep_ref, *send_refs):
-    rows = acts_ref.shape[0]
+def turn_kernel(acts_ref, turned_ref):
+    first = acts_ref.shape[1] - turned_ref.shape[0]
+    turned_ref[...] = acts_ref[:, first:].T
+
+
+def turn(acts, first):
+    rows, width = acts.shape
+    return pl.pallas_call(
+        turn_kernel,
+        out_shape=pltpu.VMEM((width - first, rows), acts.dtype),
+        in_specs=[VMEM],
+        out_specs=VMEM,
+        compiler_params=pltpu.CompilerParams(vmem_limit_bytes=VMEM_LIMIT),
+        name="turn",
+    )(acts)
+
+
+def project_rest_kernel(mine_ref, other_ref, tally_ref, shares_ref, turned_ref, keep_ref, *send_refs):
+    rows = turned_ref.shape[1]
     cands = mine_ref.shape[0] // 2
     parts = len(send_refs) + 1
     part = cands // parts
     place = lax.axis_index("feat")
     raw_dir, squares = directions(mine_ref[...] + other_ref[...], tally_ref[:, :1])
-    plain = lax.dot_general(
-        raw_dir, acts_ref[:, acts_ref.shape[1] - mine_ref.shape[1]:], (((1,), (1,)), ((), ())), preferred_element_type=jnp.float32
-    )
+    plain = jnp.dot(raw_dir, turned_ref[...], preferred_element_type=jnp.float32)
     plain = plain + shares_ref[:, :rows]
     squares = squares + shares_ref[:, rows:]
     for step, out_ref in enumerate((keep_ref,) + send_refs):
@@ -169,8 +184,8 @@
             out_ref[:, columns] = chosen
 
 
-def project_rest(mine, other, tally, shares, acts):
-    rows = acts.shape[0]
+def project_rest(mine, other, tally, shares, turned):
+    rows = turned.shape[1]
     parts = lax.axis_size("feat")
     part = jax.ShapeDtypeStruct((mine.shape[0] // 2 // parts, rows + LANES), jnp.float32)
     return pl.pallas_call(
@@ -180,7 +195,7 @@
         out_specs=(VMEM,) * parts,
         compiler_params=pltpu.CompilerParams(vmem_limit_bytes=VMEM_LIMIT),
         name="project_rest",
-    )(mine, other, tally, shares, acts)
+    )(mine, other, tally, shares, in_vmem(turned))
 
 
 def scale_kernel(*refs):
@@ -236,7 +251,7 @@
         sums = sums + dp_trade(sums, step, 0)
         rest = rest + dp_trade(rest, step, 1)
     shares, tally = project(sums, dp_trade(sums, rounds - 1, 0), acts)
-    keep, *sends = project_rest(rest, dp_trade(rest, rounds - 1, 1), tally, shares, acts)
+    keep, *sends = project_rest(rest, dp_trade(rest, rounds - 1, 1), tally, shares, turn(acts, first))
     shares = [feat_trade(sends[bits - 1], bits) for bits in range(feat - 1, 0, -1)]
     return scale([keep] + shares).T
 

time: 25.3 us -> 25 us (0.988)
  waiting for transfers between devices: 6.06 us -> 5.41 us
  Pallas kernels: 3.85 us -> 4.25 us
    ppermute x6, waiting for transfers between devices: 4.17 us -> 3.53 us  [dp_trade(): return lax.ppermute(value, ('dp', 'feat'), pairs)]
    pallas_call x0 -> x1, Pallas kernels: none -> 0.64 us  [turn(): pl.pallas_call(turn_kernel, out_shape=pltpu.VMEM((width - first, rows), a...]
  transfers between devices with their start and end apart: 9 -> 9, of which waited for: 6 -> 6; matrix products, arithmetic and copies ran while one was open for 0% -> 0% of each run, Pallas kernels for 4% -> 7%
where the time goes in v6:
time: 25 us; the launch traced here: 24.8 us
  starting transfers between devices  13.9 us (56%)
  waiting for transfers between devices  5.41 us (22%)
  Pallas kernels  4.25 us (17%)
  between operations  0.86 us (3%)
  local copies, waits for them, and re-layouts  0.34 us (1%)
    ppermute x6, starting transfers between devices, dp_trade(): return lax.ppermute(value, ('dp', 'feat'), pairs)  12 us
    ppermute x6, waiting for transfers between devices, dp_trade(): return lax.ppermute(value, ('dp', 'feat'), pairs)  3.53 us
    ppermute x3, starting transfers between devices, feat_trade(): lax.ppermute(value, 'feat', [(f, f ^ bits) for f in range(lax.axis_size('...  1.92 us
    ppermute x3, waiting for transfers between devices, feat_trade(): lax.ppermute(value, 'feat', [(f, f ^ bits) for f in range(lax.axis_size('...  1.88 us
    pallas_call x1, Pallas kernels, membership(): pl.pallas_call(member_kernel, out_shape=(jax.ShapeDtypeStruct((classes, r...  1.08 us
    pallas_call x1, Pallas kernels, scale(): pl.pallas_call(scale_kernel, out_shape=jax.ShapeDtypeStruct((part, column...  0.68 us
    pallas_call x1, Pallas kernels, project(): pl.pallas_call(project_kernel, out_shape=(jax.ShapeDtypeStruct((classes /...  0.65 us
    pallas_call x1, Pallas kernels, turn(): pl.pallas_call(turn_kernel, out_shape=pltpu.VMEM((width - first, rows), a...  0.64 us
  transfers between devices with their start and end apart: 9, of which 6 were waited for; matrix products, arithmetic and copies ran while one was open for 0% of the time, Pallas kernels for 7%

profile of v6, /device:TPU:0, one launch (start us, length us, event | category | flops | bytes accessed | tf_op | source)
XLA Modules:
  0.0 24.8 jit_solution(11133475829436099336)
XLA Ops:
  0.8 1.1 %membership.1 = (bf16[16,1024]{1,0:T(8,128)(2,1)S(1)}, f32[16,128]{1,0:T(8,128)S(1)}) custom-call(s32[1]{0:T(128)S(6)} %copy.5.counts_ref, s32[1,1024]{1,0:T(1,128)} %bitcast.3, s32[1,64]{1,0:T(1,128)} %bitcast.4), custom_call_target="tpu_custom_call" | custom-call | flops 1677721600 | tf_op jit(solution)/shard_map/membership/pallas_call | solution.py:58
  1.9 0.3 %copy-done = bf16[1024,2048]{1,0:T(8,128)(2,1)S(1)} copy-done((bf16[1024,2048]{1,0:T(8,128)(2,1)S(1)}, bf16[1024,2048]{1,0:T(8,128)(2,1)}, u32[]{:S(2)}) %copy-start) | copy-done | bytes 4194328
  2.2 0.4 %first_sums.1 = f32[16,1152]{1,0:T(8,128)S(1)} custom-call(bf16[16,1024]{1,0:T(8,128)(2,1)S(1)} %get-tuple-element.13.member_ref, f32[16,128]{1,0:T(8,128)S(1)} %get-tuple-element.14.tally_ref, bf16[1024,2048]{1,0:T(8,128)(2,1)S(1)} %copy-done), custom_call_target="tpu_custom_call" | custom-call | tf_op jit(solution)/shard_map/first_sums/pallas_call | solution.py:86
  2.6 3.0 %collective-permute-start.3 = (f32[16,1152]{1,0:T(8,128)S(1)}, f32[16,1152]{1,0:T(8,128)S(1)}, u32[]{:S(2)}, u32[]{:S(2)}) collective-permute-start(f32[16,1152]{1,0:T(8,128)S(1)} %first_sums.1), channel_id=1, source_target_pairs={{0,4},{1,17},{2,6},{3,19},{4,0},{5,21},{6,2},{7,23},{8,12},{9,25},... | collective-permute-start | bytes 221192 | tf_op jit(solution)/shard_map/ppermute | solution.py:234
  5.6 0.4 %rest_sums.1 = f32[16,1024]{1,0:T(8,128)S(1)} custom-call(bf16[16,1024]{1,0:T(8,128)(2,1)S(1)} %get-tuple-element.13.member_ref, bf16[1024,2048]{1,0:T(8,128)(2,1)S(1)} %copy-done), custom_call_target="tpu_custom_call" | custom-call | tf_op jit(solution)/shard_map/rest_sums/pallas_call | solution.py:104
  6.0 0.0 collective-permute-start
  6.0 1.9 %collective-permute-done.3 = f32[16,1152]{1,0:T(8,128)S(1)} collective-permute-done((f32[16,1152]{1,0:T(8,128)S(1)}, f32[16,1152]{1,0:T(8,128)S(1)}, u32[]{:S(2)}, u32[]{:S(2)}) %collective-permute-start.3) | collective-permute-done | bytes 73760 | tf_op jit(solution)/shard_map/ppermute | solution.py:234
  7.9 2.1 %collective-permute-start.4 = (f32[16,1152]{1,0:T(8,128)S(1)}, f32[16,1152]{1,0:T(8,128)S(1)}, u32[]{:S(2)}, u32[]{:S(2)}) collective-permute-start(f32[16,1152]{1,0:T(8,128)S(1)} %add.14), channel_id=1, source_target_pairs={{0,8},{1,5},{2,10},{3,7},{4,12},{5,1},{6,14},{7,3},{8,0},{9,13},{1... | collective-permute-start | bytes 221192 | tf_op jit(solution)/shard_map/ppermute | solution.py:234
  10.1 0.2 collective-permute-done
  10.3 2.7 %collective-permute-start.1 = (f32[16,1024]{1,0:T(8,128)S(1)}, f32[16,1024]{1,0:T(8,128)S(1)}, u32[]{:S(2)}, u32[]{:S(2)}) collective-permute-start(f32[16,1024]{1,0:T(8,128)S(1)} %add.12), channel_id=1, source_target_pairs={{0,16},{1,5},{2,18},{3,7},{4,20},{5,1},{6,22},{7,3},{8,24},{9,13},... | collective-permute-start | bytes 196616 | tf_op jit(solution)/shard_map/ppermute | solution.py:234
  12.9 2.6 %collective-permute-start.5 = (f32[16,1152]{1,0:T(8,128)S(1)}, f32[16,1152]{1,0:T(8,128)S(1)}, u32[]{:S(2)}, u32[]{:S(2)}) collective-permute-start(f32[16,1152]{1,0:T(8,128)S(1)} %add.15.mine_ref), channel_id=1, source_target_pairs={{0,16},{1,9},{2,18},{3,11},{4,20},{5,13},{6,22},{7,15},{8,24},{9,1... | collective-permute-start | bytes 221192 | tf_op jit(solution)/shard_map/ppermute | solution.py:234
  15.5 0.0 collective-permute-done.1
  15.6 1.6 %collective-permute-start.2 = (f32[16,1024]{1,0:T(8,128)S(1)}, f32[16,1024]{1,0:T(8,128)S(1)}, u32[]{:S(2)}, u32[]{:S(2)}) collective-permute-start(f32[16,1024]{1,0:T(8,128)S(1)} %add.13.mine_ref), channel_id=1, source_target_pairs={{0,8},{1,9},{2,10},{3,11},{4,12},{5,13},{6,14},{7,15},{8,0},{9,1},... | collective-permute-start | bytes 196616 | tf_op jit(solution)/shard_map/ppermute | solution.py:234
  17.2 0.6 %turn.1.turned_ref = bf16[1024,1024]{1,0:T(8,128)(2,1)S(1)} custom-call(bf16[1024,2048]{1,0:T(8,128)(2,1)S(1)} %copy-done), custom_call_target="tpu_custom_call" | custom-call | tf_op jit(solution)/shard_map/turn/pallas_call | solution.py:158
  17.8 0.4 %collective-permute-done.5.other_ref = f32[16,1152]{1,0:T(8,128)S(1)} collective-permute-done((f32[16,1152]{1,0:T(8,128)S(1)}, f32[16,1152]{1,0:T(8,128)S(1)}, u32[]{:S(2)}, u32[]{:S(2)}) %collective-permute-start.5) | collective-permute-done | bytes 73760 | tf_op jit(solution)/shard_map/ppermute | solution.py:234
  18.2 0.7 %project.1 = (f32[8,1152]{1,0:T(8,128)S(1)}, f32[16,128]{1,0:T(8,128)S(1)}) custom-call(f32[16,1152]{1,0:T(8,128)S(1)} %add.15.mine_ref, f32[16,1152]{1,0:T(8,128)S(1)} %collective-permute-done.5.other_ref, bf16[1024,2048]{1,0:T(8,128)(2,1)S(1)} %copy-done), custom_call_target="tpu_custom_call" | custom-call | tf_op jit(solution)/shard_map/project/pallas_call | solution.py:138
  18.9 1.0 %collective-permute-done.2.other_ref = f32[16,1024]{1,0:T(8,128)S(1)} collective-permute-done((f32[16,1024]{1,0:T(8,128)S(1)}, f32[16,1024]{1,0:T(8,128)S(1)}, u32[]{:S(2)}, u32[]{:S(2)}) %collective-permute-start.2) | collective-permute-done | bytes 65568 | tf_op jit(solution)/shard_map/ppermute | solution.py:234
  19.9 0.4 %project_rest.1 = (f32[2,1152]{1,0:T(2,128)S(1)}, f32[2,1152]{1,0:T(2,128)S(1)}, f32[2,1152]{1,0:T(2,128)S(1)}, f32[2,1152]{1,0:T(2,128)S(1)}) custom-call(f32[16,1024]{1,0:T(8,128)S(1)} %add.13.mine_ref, f32[16,1024]{1,0:T(8,128)S(1)} %collective-permute-done.2.other_ref, f32[16,128]{1,0:T(8,128)S(1)} %get-tuple-element.15.tally_ref, ...), custom_call_target="tpu_custom_call" | custom-call | tf_op jit(solution)/shard_map/project_rest/pallas_call | solution.py:191
  20.3 0.1 collective-permute-start.6
  20.4 1.6 %collective-permute-start.7 = (f32[2,1152]{1,0:T(2,128)S(1)}, f32[2,1152]{1,0:T(2,128)S(1)}, u32[]{:S(2)}, u32[]{:S(2)}) collective-permute-start(f32[2,1152]{1,0:T(2,128)S(1)} %get-tuple-element.19), channel_id=1, source_target_pairs={{0,2},{1,3},{2,0},{3,1},{4,6},{5,7},{6,4},{7,5},{8,10},{9,11},{10,... | collective-permute-start | bytes 27656 | tf_op jit(solution)/shard_map/ppermute | solution.py:238
  22.0 0.3 %collective-permute-start.8 = (f32[2,1152]{1,0:T(2,128)S(1)}, f32[2,1152]{1,0:T(2,128)S(1)}, u32[]{:S(2)}, u32[]{:S(2)}) collective-permute-start(f32[2,1152]{1,0:T(2,128)S(1)} %get-tuple-element.20), channel_id=1, source_target_pairs={{0,1},{1,0},{2,3},{3,2},{4,5},{5,4},{6,7},{7,6},{8,9},{9,8},{10,11... | collective-permute-start | bytes 27656 | tf_op jit(solution)/shard_map/ppermute | solution.py:238
  22.3 1.3 %collective-permute-done.6.refs_1_ = f32[2,1152]{1,0:T(2,128)S(1)} collective-permute-done((f32[2,1152]{1,0:T(2,128)S(1)}, f32[2,1152]{1,0:T(2,128)S(1)}, u32[]{:S(2)}, u32[]{:S(2)}) %collective-permute-start.6) | collective-permute-done | bytes 9248 | tf_op jit(solution)/shard_map/ppermute | solution.py:238
  23.5 0.6 %collective-permute-done.7.refs_2_ = f32[2,1152]{1,0:T(2,128)S(1)} collective-permute-done((f32[2,1152]{1,0:T(2,128)S(1)}, f32[2,1152]{1,0:T(2,128)S(1)}, u32[]{:S(2)}, u32[]{:S(2)}) %collective-permute-start.7) | collective-permute-done | bytes 9248 | tf_op jit(solution)/shard_map/ppermute | solution.py:238
  24.2 0.7 %scale.1 = f32[2,1024]{1,0:T(2,128)} custom-call(f32[2,1152]{1,0:T(2,128)S(1)} %get-tuple-element.17.refs_0_, f32[2,1152]{1,0:T(2,128)S(1)} %collective-permute-done.6.refs_1_, f32[2,1152]{1,0:T(2,128)S(1)} %collective-permute-done.7.refs_2_, f32[2,1152]{1,0:T(2,128)S(1)} %collective-permute-done.8.refs_3_), custom_call_target="tpu_custom_call" | custom-call | tf_op jit(solution)/shard_map/scale/pallas_call | solution.py:213
  (7 shorter events, 0.0 us)
Async XLA Ops:
  0.0 2.2 %copy-start = (bf16[1024,2048]{1,0:T(8,128)(2,1)S(1)}, bf16[1024,2048]{1,0:T(8,128)(2,1)}, u32[]{:S(2)}) copy-start(bf16[1024,2048]{1,0:T(8,128)(2,1)} %acts_ref.7) | copy-start | bytes 12582916
  2.6 5.3 %collective-permute-start.3 = (f32[16,1152]{1,0:T(8,128)S(1)}, f32[16,1152]{1,0:T(8,128)S(1)}, u32[]{:S(2)}, u32[]{:S(2)}) collective-permute-start(f32[16,1152]{1,0:T(8,128)S(1)} %first_sums.1), channel_id=1, source_target_pairs={{0,4},{1,17},{2,6},{3,19},{4,0},{5,21},{6,2},{7,23},{8,12},{9,25},... | collective-permute-start | bytes 221192 | tf_op jit(solution)/shard_map/ppermute | solution.py:234
  6.0 4.3 %collective-permute-start = (f32[16,1024]{1,0:T(8,128)S(1)}, f32[16,1024]{1,0:T(8,128)S(1)}, u32[]{:S(2)}, u32[]{:S(2)}) collective-permute-start(f32[16,1024]{1,0:T(8,128)S(1)} %rest_sums.1), channel_id=1, source_target_pairs={{0,4},{1,17},{2,6},{3,19},{4,0},{5,21},{6,2},{7,23},{8,12},{9,25},... | collective-permute-start | bytes 196616 | tf_op jit(solution)/shard_map/ppermute | solution.py:234
  7.9 5.0 %collective-permute-start.4 = (f32[16,1152]{1,0:T(8,128)S(1)}, f32[16,1152]{1,0:T(8,128)S(1)}, u32[]{:S(2)}, u32[]{:S(2)}) collective-permute-start(f32[16,1152]{1,0:T(8,128)S(1)} %add.14), channel_id=1, source_target_pairs={{0,8},{1,5},{2,10},{3,7},{4,12},{5,1},{6,14},{7,3},{8,0},{9,13},{1... | collective-permute-start | bytes 221192 | tf_op jit(solution)/shard_map/ppermute | solution.py:234
  10.3 5.3 %collective-permute-start.1 = (f32[16,1024]{1,0:T(8,128)S(1)}, f32[16,1024]{1,0:T(8,128)S(1)}, u32[]{:S(2)}, u32[]{:S(2)}) collective-permute-start(f32[16,1024]{1,0:T(8,128)S(1)} %add.12), channel_id=1, source_target_pairs={{0,16},{1,5},{2,18},{3,7},{4,20},{5,1},{6,22},{7,3},{8,24},{9,13},... | collective-permute-start | bytes 196616 | tf_op jit(solution)/shard_map/ppermute | solution.py:234
  12.9 5.3 %collective-permute-start.5 = (f32[16,1152]{1,0:T(8,128)S(1)}, f32[16,1152]{1,0:T(8,128)S(1)}, u32[]{:S(2)}, u32[]{:S(2)}) collective-permute-start(f32[16,1152]{1,0:T(8,128)S(1)} %add.15.mine_ref), channel_id=1, source_target_pairs={{0,16},{1,9},{2,18},{3,11},{4,20},{5,13},{6,22},{7,15},{8,24},{9,1... | collective-permute-start | bytes 221192 | tf_op jit(solution)/shard_map/ppermute | solution.py:234
  15.6 4.3 %collective-permute-start.2 = (f32[16,1024]{1,0:T(8,128)S(1)}, f32[16,1024]{1,0:T(8,128)S(1)}, u32[]{:S(2)}, u32[]{:S(2)}) collective-permute-start(f32[16,1024]{1,0:T(8,128)S(1)} %add.13.mine_ref), channel_id=1, source_target_pairs={{0,8},{1,9},{2,10},{3,11},{4,12},{5,13},{6,14},{7,15},{8,0},{9,1},... | collective-permute-start | bytes 196616 | tf_op jit(solution)/shard_map/ppermute | solution.py:234
  20.3 3.2 %collective-permute-start.6 = (f32[2,1152]{1,0:T(2,128)S(1)}, f32[2,1152]{1,0:T(2,128)S(1)}, u32[]{:S(2)}, u32[]{:S(2)}) collective-permute-start(f32[2,1152]{1,0:T(2,128)S(1)} %get-tuple-element.18), channel_id=1, source_target_pairs={{0,3},{1,2},{2,1},{3,0},{4,7},{5,6},{6,5},{7,4},{8,11},{9,10},{10,... | collective-permute-start | bytes 27656 | tf_op jit(solution)/shard_map/ppermute | solution.py:238
  20.4 3.7 %collective-permute-start.7 = (f32[2,1152]{1,0:T(2,128)S(1)}, f32[2,1152]{1,0:T(2,128)S(1)}, u32[]{:S(2)}, u32[]{:S(2)}) collective-permute-start(f32[2,1152]{1,0:T(2,128)S(1)} %get-tuple-element.19), channel_id=1, source_target_pairs={{0,2},{1,3},{2,0},{3,1},{4,6},{5,7},{6,4},{7,5},{8,10},{9,11},{10,... | collective-permute-start | bytes 27656 | tf_op jit(solution)/shard_map/ppermute | solution.py:238
  22.0 2.2 %collective-permute-start.8 = (f32[2,1152]{1,0:T(2,128)S(1)}, f32[2,1152]{1,0:T(2,128)S(1)}, u32[]{:S(2)}, u32[]{:S(2)}) collective-permute-start(f32[2,1152]{1,0:T(2,128)S(1)} %get-tuple-element.20), channel_id=1, source_target_pairs={{0,1},{1,0},{2,3},{3,2},{4,5},{5,4},{6,7},{7,6},{8,9},{9,8},{10,11... | collective-permute-start | bytes 27656 | tf_op jit(solution)/shard_map/ppermute | solution.py:238

commit v7 on v6

--- a/solution.py
+++ b/solution.py
@@ -225,7 +225,7 @@
     count = dp.bit_length() - 1
     up = list(range(count))
     even = (up, up[:1] + up[:0:-1])[half]
-    odd = up[-1:] + up[:-1]
+    odd = (up[::-1], up[1:2] + up[:1] + up[2:])[half]
     pairs = []
     for d in range(dp):
         for f in range(feat):

time: 25 us -> 25 us (level)
  no operation moved by 1% of the time
where the time goes in v7:
time: 25 us; the launch traced here: 24.8 us
  starting transfers between devices  14 us (56%)
  waiting for transfers between devices  5.3 us (21%)
  Pallas kernels  4.25 us (17%)
  between operations  0.86 us (3%)
  local copies, waits for them, and re-layouts  0.34 us (1%)
    ppermute x6, starting transfers between devices, dp_trade(): return lax.ppermute(value, ('dp', 'feat'), pairs)  12.1 us
    ppermute x6, waiting for transfers between devices, dp_trade(): return lax.ppermute(value, ('dp', 'feat'), pairs)  3.42 us
    ppermute x3, starting transfers between devices, feat_trade(): lax.ppermute(value, 'feat', [(f, f ^ bits) for f in range(lax.axis_size('...  1.92 us
    ppermute x3, waiting for transfers between devices, feat_trade(): lax.ppermute(value, 'feat', [(f, f ^ bits) for f in range(lax.axis_size('...  1.88 us
    pallas_call x1, Pallas kernels, membership(): pl.pallas_call(member_kernel, out_shape=(jax.ShapeDtypeStruct((classes, r...  1.08 us
    pallas_call x1, Pallas kernels, scale(): pl.pallas_call(scale_kernel, out_shape=jax.ShapeDtypeStruct((part, column...  0.68 us
    pallas_call x1, Pallas kernels, project(): pl.pallas_call(project_kernel, out_shape=(jax.ShapeDtypeStruct((classes /...  0.65 us
    pallas_call x1, Pallas kernels, turn(): pl.pallas_call(turn_kernel, out_shape=pltpu.VMEM((width - first, rows), a...  0.64 us
  transfers between devices with their start and end apart: 9, of which 6 were waited for; matrix products, arithmetic and copies ran while one was open for 0% of the time, Pallas kernels for 7%

profile of v7, /device:TPU:0, one launch (start us, length us, event | category | flops | bytes accessed | tf_op | source)
XLA Modules:
  0.0 24.8 jit_solution(3421199126388979621)
XLA Ops:
  0.8 1.1 %membership.1 = (bf16[16,1024]{1,0:T(8,128)(2,1)S(1)}, f32[16,128]{1,0:T(8,128)S(1)}) custom-call(s32[1]{0:T(128)S(6)} %copy.5.counts_ref, s32[1,1024]{1,0:T(1,128)} %bitcast.3, s32[1,64]{1,0:T(1,128)} %bitcast.4), custom_call_target="tpu_custom_call" | custom-call | flops 1677721600 | tf_op jit(solution)/shard_map/membership/pallas_call | solution.py:58
  1.9 0.3 %copy-done = bf16[1024,2048]{1,0:T(8,128)(2,1)S(1)} copy-done((bf16[1024,2048]{1,0:T(8,128)(2,1)S(1)}, bf16[1024,2048]{1,0:T(8,128)(2,1)}, u32[]{:S(2)}) %copy-start) | copy-done | bytes 4194328
  2.2 0.4 %first_sums.1 = f32[16,1152]{1,0:T(8,128)S(1)} custom-call(bf16[16,1024]{1,0:T(8,128)(2,1)S(1)} %get-tuple-element.13.member_ref, f32[16,128]{1,0:T(8,128)S(1)} %get-tuple-element.14.tally_ref, bf16[1024,2048]{1,0:T(8,128)(2,1)S(1)} %copy-done), custom_call_target="tpu_custom_call" | custom-call | tf_op jit(solution)/shard_map/first_sums/pallas_call | solution.py:86
  2.6 3.0 %collective-permute-start.3 = (f32[16,1152]{1,0:T(8,128)S(1)}, f32[16,1152]{1,0:T(8,128)S(1)}, u32[]{:S(2)}, u32[]{:S(2)}) collective-permute-start(f32[16,1152]{1,0:T(8,128)S(1)} %first_sums.1), channel_id=1, source_target_pairs={{0,4},{1,17},{2,6},{3,19},{4,0},{5,21},{6,2},{7,23},{8,12},{9,25},... | collective-permute-start | bytes 221192 | tf_op jit(solution)/shard_map/ppermute | solution.py:234
  5.6 0.4 %rest_sums.1 = f32[16,1024]{1,0:T(8,128)S(1)} custom-call(bf16[16,1024]{1,0:T(8,128)(2,1)S(1)} %get-tuple-element.13.member_ref, bf16[1024,2048]{1,0:T(8,128)(2,1)S(1)} %copy-done), custom_call_target="tpu_custom_call" | custom-call | tf_op jit(solution)/shard_map/rest_sums/pallas_call | solution.py:104
  6.0 0.0 collective-permute-start
  6.0 1.9 %collective-permute-done.3 = f32[16,1152]{1,0:T(8,128)S(1)} collective-permute-done((f32[16,1152]{1,0:T(8,128)S(1)}, f32[16,1152]{1,0:T(8,128)S(1)}, u32[]{:S(2)}, u32[]{:S(2)}) %collective-permute-start.3) | collective-permute-done | bytes 73760 | tf_op jit(solution)/shard_map/ppermute | solution.py:234
  7.9 2.1 %collective-permute-start.4 = (f32[16,1152]{1,0:T(8,128)S(1)}, f32[16,1152]{1,0:T(8,128)S(1)}, u32[]{:S(2)}, u32[]{:S(2)}) collective-permute-start(f32[16,1152]{1,0:T(8,128)S(1)} %add.14), channel_id=1, source_target_pairs={{0,8},{1,9},{2,10},{3,11},{4,12},{5,13},{6,14},{7,15},{8,0},{9,1},... | collective-permute-start | bytes 221192 | tf_op jit(solution)/shard_map/ppermute | solution.py:234
  10.1 0.2 collective-permute-done
  10.3 2.7 %collective-permute-start.1 = (f32[16,1024]{1,0:T(8,128)S(1)}, f32[16,1024]{1,0:T(8,128)S(1)}, u32[]{:S(2)}, u32[]{:S(2)}) collective-permute-start(f32[16,1024]{1,0:T(8,128)S(1)} %add.12), channel_id=1, source_target_pairs={{0,16},{1,5},{2,18},{3,7},{4,20},{5,1},{6,22},{7,3},{8,24},{9,13},... | collective-permute-start | bytes 196616 | tf_op jit(solution)/shard_map/ppermute | solution.py:234
  12.9 0.0 collective-permute-done.4
  12.9 2.6 %collective-permute-start.5 = (f32[16,1152]{1,0:T(8,128)S(1)}, f32[16,1152]{1,0:T(8,128)S(1)}, u32[]{:S(2)}, u32[]{:S(2)}) collective-permute-start(f32[16,1152]{1,0:T(8,128)S(1)} %add.15.mine_ref), channel_id=1, source_target_pairs={{0,16},{1,5},{2,18},{3,7},{4,20},{5,1},{6,22},{7,3},{8,24},{9,13},... | collective-permute-start | bytes 221192 | tf_op jit(solution)/shard_map/ppermute | solution.py:234
  15.5 1.7 %collective-permute-start.2 = (f32[16,1024]{1,0:T(8,128)S(1)}, f32[16,1024]{1,0:T(8,128)S(1)}, u32[]{:S(2)}, u32[]{:S(2)}) collective-permute-start(f32[16,1024]{1,0:T(8,128)S(1)} %add.13.mine_ref), channel_id=1, source_target_pairs={{0,8},{1,17},{2,10},{3,19},{4,12},{5,21},{6,14},{7,23},{8,0},{9,25... | collective-permute-start | bytes 196616 | tf_op jit(solution)/shard_map/ppermute | solution.py:234
  17.3 0.6 %turn.1.turned_ref = bf16[1024,1024]{1,0:T(8,128)(2,1)S(1)} custom-call(bf16[1024,2048]{1,0:T(8,128)(2,1)S(1)} %copy-done), custom_call_target="tpu_custom_call" | custom-call | tf_op jit(solution)/shard_map/turn/pallas_call | solution.py:158
  17.9 0.4 %collective-permute-done.5.other_ref = f32[16,1152]{1,0:T(8,128)S(1)} collective-permute-done((f32[16,1152]{1,0:T(8,128)S(1)}, f32[16,1152]{1,0:T(8,128)S(1)}, u32[]{:S(2)}, u32[]{:S(2)}) %collective-permute-start.5) | collective-permute-done | bytes 73760 | tf_op jit(solution)/shard_map/ppermute | solution.py:234
  18.3 0.7 %project.1 = (f32[8,1152]{1,0:T(8,128)S(1)}, f32[16,128]{1,0:T(8,128)S(1)}) custom-call(f32[16,1152]{1,0:T(8,128)S(1)} %add.15.mine_ref, f32[16,1152]{1,0:T(8,128)S(1)} %collective-permute-done.5.other_ref, bf16[1024,2048]{1,0:T(8,128)(2,1)S(1)} %copy-done), custom_call_target="tpu_custom_call" | custom-call | tf_op jit(solution)/shard_map/project/pallas_call | solution.py:138
  18.9 0.9 %collective-permute-done.2.other_ref = f32[16,1024]{1,0:T(8,128)S(1)} collective-permute-done((f32[16,1024]{1,0:T(8,128)S(1)}, f32[16,1024]{1,0:T(8,128)S(1)}, u32[]{:S(2)}, u32[]{:S(2)}) %collective-permute-start.2) | collective-permute-done | bytes 65568 | tf_op jit(solution)/shard_map/ppermute | solution.py:234
  19.9 0.4 %project_rest.1 = (f32[2,1152]{1,0:T(2,128)S(1)}, f32[2,1152]{1,0:T(2,128)S(1)}, f32[2,1152]{1,0:T(2,128)S(1)}, f32[2,1152]{1,0:T(2,128)S(1)}) custom-call(f32[16,1024]{1,0:T(8,128)S(1)} %add.13.mine_ref, f32[16,1024]{1,0:T(8,128)S(1)} %collective-permute-done.2.other_ref, f32[16,128]{1,0:T(8,128)S(1)} %get-tuple-element.15.tally_ref, ...), custom_call_target="tpu_custom_call" | custom-call | tf_op jit(solution)/shard_map/project_rest/pallas_call | solution.py:191
  20.3 0.1 collective-permute-start.6
  20.4 1.6 %collective-permute-start.7 = (f32[2,1152]{1,0:T(2,128)S(1)}, f32[2,1152]{1,0:T(2,128)S(1)}, u32[]{:S(2)}, u32[]{:S(2)}) collective-permute-start(f32[2,1152]{1,0:T(2,128)S(1)} %get-tuple-element.19), channel_id=1, source_target_pairs={{0,2},{1,3},{2,0},{3,1},{4,6},{5,7},{6,4},{7,5},{8,10},{9,11},{10,... | collective-permute-start | bytes 27656 | tf_op jit(solution)/shard_map/ppermute | solution.py:238
  22.0 0.3 %collective-permute-start.8 = (f32[2,1152]{1,0:T(2,128)S(1)}, f32[2,1152]{1,0:T(2,128)S(1)}, u32[]{:S(2)}, u32[]{:S(2)}) collective-permute-start(f32[2,1152]{1,0:T(2,128)S(1)} %get-tuple-element.20), channel_id=1, source_target_pairs={{0,1},{1,0},{2,3},{3,2},{4,5},{5,4},{6,7},{7,6},{8,9},{9,8},{10,11... | collective-permute-start | bytes 27656 | tf_op jit(solution)/shard_map/ppermute | solution.py:238
  22.3 1.3 %collective-permute-done.6.refs_1_ = f32[2,1152]{1,0:T(2,128)S(1)} collective-permute-done((f32[2,1152]{1,0:T(2,128)S(1)}, f32[2,1152]{1,0:T(2,128)S(1)}, u32[]{:S(2)}, u32[]{:S(2)}) %collective-permute-start.6) | collective-permute-done | bytes 9248 | tf_op jit(solution)/shard_map/ppermute | solution.py:238
  23.5 0.6 %collective-permute-done.7.refs_2_ = f32[2,1152]{1,0:T(2,128)S(1)} collective-permute-done((f32[2,1152]{1,0:T(2,128)S(1)}, f32[2,1152]{1,0:T(2,128)S(1)}, u32[]{:S(2)}, u32[]{:S(2)}) %collective-permute-start.7) | collective-permute-done | bytes 9248 | tf_op jit(solution)/shard_map/ppermute | solution.py:238
  24.1 0.7 %scale.1 = f32[2,1024]{1,0:T(2,128)} custom-call(f32[2,1152]{1,0:T(2,128)S(1)} %get-tuple-element.17.refs_0_, f32[2,1152]{1,0:T(2,128)S(1)} %collective-permute-done.6.refs_1_, f32[2,1152]{1,0:T(2,128)S(1)} %collective-permute-done.7.refs_2_, f32[2,1152]{1,0:T(2,128)S(1)} %collective-permute-done.8.refs_3_), custom_call_target="tpu_custom_call" | custom-call | tf_op jit(solution)/shard_map/scale/pallas_call | solution.py:213
  (7 shorter events, 0.0 us)
Async XLA Ops:
  0.0 2.2 %copy-start = (bf16[1024,2048]{1,0:T(8,128)(2,1)S(1)}, bf16[1024,2048]{1,0:T(8,128)(2,1)}, u32[]{:S(2)}) copy-start(bf16[1024,2048]{1,0:T(8,128)(2,1)} %acts_ref.7) | copy-start | bytes 12582916
  2.6 5.3 %collective-permute-start.3 = (f32[16,1152]{1,0:T(8,128)S(1)}, f32[16,1152]{1,0:T(8,128)S(1)}, u32[]{:S(2)}, u32[]{:S(2)}) collective-permute-start(f32[16,1152]{1,0:T(8,128)S(1)} %first_sums.1), channel_id=1, source_target_pairs={{0,4},{1,17},{2,6},{3,19},{4,0},{5,21},{6,2},{7,23},{8,12},{9,25},... | collective-permute-start | bytes 221192 | tf_op jit(solution)/shard_map/ppermute | solution.py:234
  6.0 4.3 %collective-permute-start = (f32[16,1024]{1,0:T(8,128)S(1)}, f32[16,1024]{1,0:T(8,128)S(1)}, u32[]{:S(2)}, u32[]{:S(2)}) collective-permute-start(f32[16,1024]{1,0:T(8,128)S(1)} %rest_sums.1), channel_id=1, source_target_pairs={{0,4},{1,9},{2,6},{3,11},{4,0},{5,13},{6,2},{7,15},{8,12},{9,1},{1... | collective-permute-start | bytes 196616 | tf_op jit(solution)/shard_map/ppermute | solution.py:234
  7.9 5.0 %collective-permute-start.4 = (f32[16,1152]{1,0:T(8,128)S(1)}, f32[16,1152]{1,0:T(8,128)S(1)}, u32[]{:S(2)}, u32[]{:S(2)}) collective-permute-start(f32[16,1152]{1,0:T(8,128)S(1)} %add.14), channel_id=1, source_target_pairs={{0,8},{1,9},{2,10},{3,11},{4,12},{5,13},{6,14},{7,15},{8,0},{9,1},... | collective-permute-start | bytes 221192 | tf_op jit(solution)/shard_map/ppermute | solution.py:234
  10.3 5.3 %collective-permute-start.1 = (f32[16,1024]{1,0:T(8,128)S(1)}, f32[16,1024]{1,0:T(8,128)S(1)}, u32[]{:S(2)}, u32[]{:S(2)}) collective-permute-start(f32[16,1024]{1,0:T(8,128)S(1)} %add.12), channel_id=1, source_target_pairs={{0,16},{1,5},{2,18},{3,7},{4,20},{5,1},{6,22},{7,3},{8,24},{9,13},... | collective-permute-start | bytes 196616 | tf_op jit(solution)/shard_map/ppermute | solution.py:234
  12.9 5.4 %collective-permute-start.5 = (f32[16,1152]{1,0:T(8,128)S(1)}, f32[16,1152]{1,0:T(8,128)S(1)}, u32[]{:S(2)}, u32[]{:S(2)}) collective-permute-start(f32[16,1152]{1,0:T(8,128)S(1)} %add.15.mine_ref), channel_id=1, source_target_pairs={{0,16},{1,5},{2,18},{3,7},{4,20},{5,1},{6,22},{7,3},{8,24},{9,13},... | collective-permute-start | bytes 221192 | tf_op jit(solution)/shard_map/ppermute | solution.py:234
  15.5 4.3 %collective-permute-start.2 = (f32[16,1024]{1,0:T(8,128)S(1)}, f32[16,1024]{1,0:T(8,128)S(1)}, u32[]{:S(2)}, u32[]{:S(2)}) collective-permute-start(f32[16,1024]{1,0:T(8,128)S(1)} %add.13.mine_ref), channel_id=1, source_target_pairs={{0,8},{1,17},{2,10},{3,19},{4,12},{5,21},{6,14},{7,23},{8,0},{9,25... | collective-permute-start | bytes 196616 | tf_op jit(solution)/shard_map/ppermute | solution.py:234
  20.3 3.2 %collective-permute-start.6 = (f32[2,1152]{1,0:T(2,128)S(1)}, f32[2,1152]{1,0:T(2,128)S(1)}, u32[]{:S(2)}, u32[]{:S(2)}) collective-permute-start(f32[2,1152]{1,0:T(2,128)S(1)} %get-tuple-element.18), channel_id=1, source_target_pairs={{0,3},{1,2},{2,1},{3,0},{4,7},{5,6},{6,5},{7,4},{8,11},{9,10},{10,... | collective-permute-start | bytes 27656 | tf_op jit(solution)/shard_map/ppermute | solution.py:238
  20.4 3.7 %collective-permute-start.7 = (f32[2,1152]{1,0:T(2,128)S(1)}, f32[2,1152]{1,0:T(2,128)S(1)}, u32[]{:S(2)}, u32[]{:S(2)}) collective-permute-start(f32[2,1152]{1,0:T(2,128)S(1)} %get-tuple-element.19), channel_id=1, source_target_pairs={{0,2},{1,3},{2,0},{3,1},{4,6},{5,7},{6,4},{7,5},{8,10},{9,11},{10,... | collective-permute-start | bytes 27656 | tf_op jit(solution)/shard_map/ppermute | solution.py:238
  22.0 2.2 %collective-permute-start.8 = (f32[2,1152]{1,0:T(2,128)S(1)}, f32[2,1152]{1,0:T(2,128)S(1)}, u32[]{:S(2)}, u32[]{:S(2)}) collective-permute-start(f32[2,1152]{1,0:T(2,128)S(1)} %get-tuple-element.20), channel_id=1, source_target_pairs={{0,1},{1,0},{2,3},{3,2},{4,5},{5,4},{6,7},{7,6},{8,9},{9,8},{10,11... | collective-permute-start | bytes 27656 | tf_op jit(solution)/shard_map/ppermute | solution.py:238

commit v8 on v6

--- a/solution.py
+++ b/solution.py
@@ -171,10 +171,13 @@
     parts = len(send_refs) + 1
     part = cands // parts
     place = lax.axis_index("feat")
-    raw_dir, squares = directions(mine_ref[...] + other_ref[...], tally_ref[:, :1])
-    plain = jnp.dot(raw_dir, turned_ref[...], preferred_element_type=jnp.float32)
-    plain = plain + shares_ref[:, :rows]
-    squares = squares + shares_ref[:, rows:]
+    plain, squares = shares_ref[:, :rows], shares_ref[:, rows:]
+    tall = turned_ref.shape[0] // 4
+    for piece in range(4):
+        here = slice(piece * tall, (piece + 1) * tall)
+        raw_dir, piece_squares = directions(mine_ref[:, here] + other_ref[:, here], tally_ref[:, :1])
+        plain = plain + jnp.dot(raw_dir, turned_ref[here, :], preferred_element_type=jnp.float32)
+        squares = squares + piece_squares
     for step, out_ref in enumerate((keep_ref,) + send_refs):
         for value, columns in ((plain, slice(0, rows)), (squares, slice(rows, rows + LANES))):
             chosen = value[:part]

time: 25 us -> 25 us (level)
  no operation moved by 1% of the time
where the time goes in v8:
time: 25 us; the launch traced here: 24.8 us
  starting transfers between devices  13.9 us (56%)
  waiting for transfers between devices  5.41 us (22%)
  Pallas kernels  4.25 us (17%)
  between operations  0.86 us (3%)
  local copies, waits for them, and re-layouts  0.34 us (1%)
    ppermute x6, starting transfers between devices, dp_trade(): return lax.ppermute(value, ('dp', 'feat'), pairs)  12 us
    ppermute x6, waiting for transfers between devices, dp_trade(): return lax.ppermute(value, ('dp', 'feat'), pairs)  3.53 us
    ppermute x3, starting transfers between devices, feat_trade(): lax.ppermute(value, 'feat', [(f, f ^ bits) for f in range(lax.axis_size('...  1.92 us
    ppermute x3, waiting for transfers between devices, feat_trade(): lax.ppermute(value, 'feat', [(f, f ^ bits) for f in range(lax.axis_size('...  1.88 us
    pallas_call x1, Pallas kernels, membership(): pl.pallas_call(member_kernel, out_shape=(jax.ShapeDtypeStruct((classes, r...  1.08 us
    pallas_call x1, Pallas kernels, scale(): pl.pallas_call(scale_kernel, out_shape=jax.ShapeDtypeStruct((part, column...  0.68 us
    pallas_call x1, Pallas kernels, project(): pl.pallas_call(project_kernel, out_shape=(jax.ShapeDtypeStruct((classes /...  0.65 us
    pallas_call x1, Pallas kernels, turn(): pl.pallas_call(turn_kernel, out_shape=pltpu.VMEM((width - first, rows), a...  0.64 us
  transfers between devices with their start and end apart: 9, of which 6 were waited for; matrix products, arithmetic and copies ran while one was open for 0% of the time, Pallas kernels for 7%

profile of v8, /device:TPU:0, one launch (start us, length us, event | category | flops | bytes accessed | tf_op | source)
XLA Modules:
  0.0 24.8 jit_solution(10139159198517643046)
XLA Ops:
  0.8 1.1 %membership.1 = (bf16[16,1024]{1,0:T(8,128)(2,1)S(1)}, f32[16,128]{1,0:T(8,128)S(1)}) custom-call(s32[1]{0:T(128)S(6)} %copy.5.counts_ref, s32[1,1024]{1,0:T(1,128)} %bitcast.3, s32[1,64]{1,0:T(1,128)} %bitcast.4), custom_call_target="tpu_custom_call" | custom-call | flops 1677721600 | tf_op jit(solution)/shard_map/membership/pallas_call | solution.py:58
  1.9 0.3 %copy-done = bf16[1024,2048]{1,0:T(8,128)(2,1)S(1)} copy-done((bf16[1024,2048]{1,0:T(8,128)(2,1)S(1)}, bf16[1024,2048]{1,0:T(8,128)(2,1)}, u32[]{:S(2)}) %copy-start) | copy-done | bytes 4194328
  2.2 0.4 %first_sums.1 = f32[16,1152]{1,0:T(8,128)S(1)} custom-call(bf16[16,1024]{1,0:T(8,128)(2,1)S(1)} %get-tuple-element.13.member_ref, f32[16,128]{1,0:T(8,128)S(1)} %get-tuple-element.14.tally_ref, bf16[1024,2048]{1,0:T(8,128)(2,1)S(1)} %copy-done), custom_call_target="tpu_custom_call" | custom-call | tf_op jit(solution)/shard_map/first_sums/pallas_call | solution.py:86
  2.6 3.0 %collective-permute-start.3 = (f32[16,1152]{1,0:T(8,128)S(1)}, f32[16,1152]{1,0:T(8,128)S(1)}, u32[]{:S(2)}, u32[]{:S(2)}) collective-permute-start(f32[16,1152]{1,0:T(8,128)S(1)} %first_sums.1), channel_id=1, source_target_pairs={{0,4},{1,17},{2,6},{3,19},{4,0},{5,21},{6,2},{7,23},{8,12},{9,25},... | collective-permute-start | bytes 221192 | tf_op jit(solution)/shard_map/ppermute | solution.py:237
  5.6 0.4 %rest_sums.1 = f32[16,1024]{1,0:T(8,128)S(1)} custom-call(bf16[16,1024]{1,0:T(8,128)(2,1)S(1)} %get-tuple-element.13.member_ref, bf16[1024,2048]{1,0:T(8,128)(2,1)S(1)} %copy-done), custom_call_target="tpu_custom_call" | custom-call | tf_op jit(solution)/shard_map/rest_sums/pallas_call | solution.py:104
  6.0 0.0 collective-permute-start
  6.0 1.9 %collective-permute-done.3 = f32[16,1152]{1,0:T(8,128)S(1)} collective-permute-done((f32[16,1152]{1,0:T(8,128)S(1)}, f32[16,1152]{1,0:T(8,128)S(1)}, u32[]{:S(2)}, u32[]{:S(2)}) %collective-permute-start.3) | collective-permute-done | bytes 73760 | tf_op jit(solution)/shard_map/ppermute | solution.py:237
  7.9 2.1 %collective-permute-start.4 = (f32[16,1152]{1,0:T(8,128)S(1)}, f32[16,1152]{1,0:T(8,128)S(1)}, u32[]{:S(2)}, u32[]{:S(2)}) collective-permute-start(f32[16,1152]{1,0:T(8,128)S(1)} %add.14), channel_id=1, source_target_pairs={{0,8},{1,5},{2,10},{3,7},{4,12},{5,1},{6,14},{7,3},{8,0},{9,13},{1... | collective-permute-start | bytes 221192 | tf_op jit(solution)/shard_map/ppermute | solution.py:237
  10.1 0.2 collective-permute-done
  10.3 2.7 %collective-permute-start.1 = (f32[16,1024]{1,0:T(8,128)S(1)}, f32[16,1024]{1,0:T(8,128)S(1)}, u32[]{:S(2)}, u32[]{:S(2)}) collective-permute-start(f32[16,1024]{1,0:T(8,128)S(1)} %add.12), channel_id=1, source_target_pairs={{0,16},{1,5},{2,18},{3,7},{4,20},{5,1},{6,22},{7,3},{8,24},{9,13},... | collective-permute-start | bytes 196616 | tf_op jit(solution)/shard_map/ppermute | solution.py:237
  12.9 2.6 %collective-permute-start.5 = (f32[16,1152]{1,0:T(8,128)S(1)}, f32[16,1152]{1,0:T(8,128)S(1)}, u32[]{:S(2)}, u32[]{:S(2)}) collective-permute-start(f32[16,1152]{1,0:T(8,128)S(1)} %add.15.mine_ref), channel_id=1, source_target_pairs={{0,16},{1,9},{2,18},{3,11},{4,20},{5,13},{6,22},{7,15},{8,24},{9,1... | collective-permute-start | bytes 221192 | tf_op jit(solution)/shard_map/ppermute | solution.py:237
  15.5 0.0 collective-permute-done.1
  15.6 1.6 %collective-permute-start.2 = (f32[16,1024]{1,0:T(8,128)S(1)}, f32[16,1024]{1,0:T(8,128)S(1)}, u32[]{:S(2)}, u32[]{:S(2)}) collective-permute-start(f32[16,1024]{1,0:T(8,128)S(1)} %add.13.mine_ref), channel_id=1, source_target_pairs={{0,8},{1,9},{2,10},{3,11},{4,12},{5,13},{6,14},{7,15},{8,0},{9,1},... | collective-permute-start | bytes 196616 | tf_op jit(solution)/shard_map/ppermute | solution.py:237
  17.2 0.6 %turn.1.turned_ref = bf16[1024,1024]{1,0:T(8,128)(2,1)S(1)} custom-call(bf16[1024,2048]{1,0:T(8,128)(2,1)S(1)} %copy-done), custom_call_target="tpu_custom_call" | custom-call | tf_op jit(solution)/shard_map/turn/pallas_call | solution.py:158
  17.8 0.4 %collective-permute-done.5.other_ref = f32[16,1152]{1,0:T(8,128)S(1)} collective-permute-done((f32[16,1152]{1,0:T(8,128)S(1)}, f32[16,1152]{1,0:T(8,128)S(1)}, u32[]{:S(2)}, u32[]{:S(2)}) %collective-permute-start.5) | collective-permute-done | bytes 73760 | tf_op jit(solution)/shard_map/ppermute | solution.py:237
  18.2 0.7 %project.1 = (f32[8,1152]{1,0:T(8,128)S(1)}, f32[16,128]{1,0:T(8,128)S(1)}) custom-call(f32[16,1152]{1,0:T(8,128)S(1)} %add.15.mine_ref, f32[16,1152]{1,0:T(8,128)S(1)} %collective-permute-done.5.other_ref, bf16[1024,2048]{1,0:T(8,128)(2,1)S(1)} %copy-done), custom_call_target="tpu_custom_call" | custom-call | tf_op jit(solution)/shard_map/project/pallas_call | solution.py:138
  18.9 1.0 %collective-permute-done.2.other_ref = f32[16,1024]{1,0:T(8,128)S(1)} collective-permute-done((f32[16,1024]{1,0:T(8,128)S(1)}, f32[16,1024]{1,0:T(8,128)S(1)}, u32[]{:S(2)}, u32[]{:S(2)}) %collective-permute-start.2) | collective-permute-done | bytes 65568 | tf_op jit(solution)/shard_map/ppermute | solution.py:237
  19.9 0.4 %project_rest.1 = (f32[2,1152]{1,0:T(2,128)S(1)}, f32[2,1152]{1,0:T(2,128)S(1)}, f32[2,1152]{1,0:T(2,128)S(1)}, f32[2,1152]{1,0:T(2,128)S(1)}) custom-call(f32[16,1024]{1,0:T(8,128)S(1)} %add.13.mine_ref, f32[16,1024]{1,0:T(8,128)S(1)} %collective-permute-done.2.other_ref, f32[16,128]{1,0:T(8,128)S(1)} %get-tuple-element.15.tally_ref, ...), custom_call_target="tpu_custom_call" | custom-call | tf_op jit(solution)/shard_map/project_rest/pallas_call | solution.py:194
  20.3 0.1 collective-permute-start.6
  20.4 1.6 %collective-permute-start.7 = (f32[2,1152]{1,0:T(2,128)S(1)}, f32[2,1152]{1,0:T(2,128)S(1)}, u32[]{:S(2)}, u32[]{:S(2)}) collective-permute-start(f32[2,1152]{1,0:T(2,128)S(1)} %get-tuple-element.19), channel_id=1, source_target_pairs={{0,2},{1,3},{2,0},{3,1},{4,6},{5,7},{6,4},{7,5},{8,10},{9,11},{10,... | collective-permute-start | bytes 27656 | tf_op jit(solution)/shard_map/ppermute | solution.py:241
  22.0 0.3 %collective-permute-start.8 = (f32[2,1152]{1,0:T(2,128)S(1)}, f32[2,1152]{1,0:T(2,128)S(1)}, u32[]{:S(2)}, u32[]{:S(2)}) collective-permute-start(f32[2,1152]{1,0:T(2,128)S(1)} %get-tuple-element.20), channel_id=1, source_target_pairs={{0,1},{1,0},{2,3},{3,2},{4,5},{5,4},{6,7},{7,6},{8,9},{9,8},{10,11... | collective-permute-start | bytes 27656 | tf_op jit(solution)/shard_map/ppermute | solution.py:241
  22.3 1.3 %collective-permute-done.6.refs_1_ = f32[2,1152]{1,0:T(2,128)S(1)} collective-permute-done((f32[2,1152]{1,0:T(2,128)S(1)}, f32[2,1152]{1,0:T(2,128)S(1)}, u32[]{:S(2)}, u32[]{:S(2)}) %collective-permute-start.6) | collective-permute-done | bytes 9248 | tf_op jit(solution)/shard_map/ppermute | solution.py:241
  23.5 0.6 %collective-permute-done.7.refs_2_ = f32[2,1152]{1,0:T(2,128)S(1)} collective-permute-done((f32[2,1152]{1,0:T(2,128)S(1)}, f32[2,1152]{1,0:T(2,128)S(1)}, u32[]{:S(2)}, u32[]{:S(2)}) %collective-permute-start.7) | collective-permute-done | bytes 9248 | tf_op jit(solution)/shard_map/ppermute | solution.py:241
  24.2 0.7 %scale.1 = f32[2,1024]{1,0:T(2,128)} custom-call(f32[2,1152]{1,0:T(2,128)S(1)} %get-tuple-element.17.refs_0_, f32[2,1152]{1,0:T(2,128)S(1)} %collective-permute-done.6.refs_1_, f32[2,1152]{1,0:T(2,128)S(1)} %collective-permute-done.7.refs_2_, f32[2,1152]{1,0:T(2,128)S(1)} %collective-permute-done.8.refs_3_), custom_call_target="tpu_custom_call" | custom-call | tf_op jit(solution)/shard_map/scale/pallas_call | solution.py:216
  (7 shorter events, 0.0 us)
Async XLA Ops:
  0.0 2.2 %copy-start = (bf16[1024,2048]{1,0:T(8,128)(2,1)S(1)}, bf16[1024,2048]{1,0:T(8,128)(2,1)}, u32[]{:S(2)}) copy-start(bf16[1024,2048]{1,0:T(8,128)(2,1)} %acts_ref.7) | copy-start | bytes 12582916
  2.6 5.3 %collective-permute-start.3 = (f32[16,1152]{1,0:T(8,128)S(1)}, f32[16,1152]{1,0:T(8,128)S(1)}, u32[]{:S(2)}, u32[]{:S(2)}) collective-permute-start(f32[16,1152]{1,0:T(8,128)S(1)} %first_sums.1), channel_id=1, source_target_pairs={{0,4},{1,17},{2,6},{3,19},{4,0},{5,21},{6,2},{7,23},{8,12},{9,25},... | collective-permute-start | bytes 221192 | tf_op jit(solution)/shard_map/ppermute | solution.py:237
  6.0 4.3 %collective-permute-start = (f32[16,1024]{1,0:T(8,128)S(1)}, f32[16,1024]{1,0:T(8,128)S(1)}, u32[]{:S(2)}, u32[]{:S(2)}) collective-permute-start(f32[16,1024]{1,0:T(8,128)S(1)} %rest_sums.1), channel_id=1, source_target_pairs={{0,4},{1,17},{2,6},{3,19},{4,0},{5,21},{6,2},{7,23},{8,12},{9,25},... | collective-permute-start | bytes 196616 | tf_op jit(solution)/shard_map/ppermute | solution.py:237
  7.9 5.0 %collective-permute-start.4 = (f32[16,1152]{1,0:T(8,128)S(1)}, f32[16,1152]{1,0:T(8,128)S(1)}, u32[]{:S(2)}, u32[]{:S(2)}) collective-permute-start(f32[16,1152]{1,0:T(8,128)S(1)} %add.14), channel_id=1, source_target_pairs={{0,8},{1,5},{2,10},{3,7},{4,12},{5,1},{6,14},{7,3},{8,0},{9,13},{1... | collective-permute-start | bytes 221192 | tf_op jit(solution)/shard_map/ppermute | solution.py:237
  10.3 5.3 %collective-permute-start.1 = (f32[16,1024]{1,0:T(8,128)S(1)}, f32[16,1024]{1,0:T(8,128)S(1)}, u32[]{:S(2)}, u32[]{:S(2)}) collective-permute-start(f32[16,1024]{1,0:T(8,128)S(1)} %add.12), channel_id=1, source_target_pairs={{0,16},{1,5},{2,18},{3,7},{4,20},{5,1},{6,22},{7,3},{8,24},{9,13},... | collective-permute-start | bytes 196616 | tf_op jit(solution)/shard_map/ppermute | solution.py:237
  12.9 5.3 %collective-permute-start.5 = (f32[16,1152]{1,0:T(8,128)S(1)}, f32[16,1152]{1,0:T(8,128)S(1)}, u32[]{:S(2)}, u32[]{:S(2)}) collective-permute-start(f32[16,1152]{1,0:T(8,128)S(1)} %add.15.mine_ref), channel_id=1, source_target_pairs={{0,16},{1,9},{2,18},{3,11},{4,20},{5,13},{6,22},{7,15},{8,24},{9,1... | collective-permute-start | bytes 221192 | tf_op jit(solution)/shard_map/ppermute | solution.py:237
  15.6 4.3 %collective-permute-start.2 = (f32[16,1024]{1,0:T(8,128)S(1)}, f32[16,1024]{1,0:T(8,128)S(1)}, u32[]{:S(2)}, u32[]{:S(2)}) collective-permute-start(f32[16,1024]{1,0:T(8,128)S(1)} %add.13.mine_ref), channel_id=1, source_target_pairs={{0,8},{1,9},{2,10},{3,11},{4,12},{5,13},{6,14},{7,15},{8,0},{9,1},... | collective-permute-start | bytes 196616 | tf_op jit(solution)/shard_map/ppermute | solution.py:237
  20.3 3.2 %collective-permute-start.6 = (f32[2,1152]{1,0:T(2,128)S(1)}, f32[2,1152]{1,0:T(2,128)S(1)}, u32[]{:S(2)}, u32[]{:S(2)}) collective-permute-start(f32[2,1152]{1,0:T(2,128)S(1)} %get-tuple-element.18), channel_id=1, source_target_pairs={{0,3},{1,2},{2,1},{3,0},{4,7},{5,6},{6,5},{7,4},{8,11},{9,10},{10,... | collective-permute-start | bytes 27656 | tf_op jit(solution)/shard_map/ppermute | solution.py:241
  20.4 3.7 %collective-permute-start.7 = (f32[2,1152]{1,0:T(2,128)S(1)}, f32[2,1152]{1,0:T(2,128)S(1)}, u32[]{:S(2)}, u32[]{:S(2)}) collective-permute-start(f32[2,1152]{1,0:T(2,128)S(1)} %get-tuple-element.19), channel_id=1, source_target_pairs={{0,2},{1,3},{2,0},{3,1},{4,6},{5,7},{6,4},{7,5},{8,10},{9,11},{10,... | collective-permute-start | bytes 27656 | tf_op jit(solution)/shard_map/ppermute | solution.py:241
  22.0 2.2 %collective-permute-start.8 = (f32[2,1152]{1,0:T(2,128)S(1)}, f32[2,1152]{1,0:T(2,128)S(1)}, u32[]{:S(2)}, u32[]{:S(2)}) collective-permute-start(f32[2,1152]{1,0:T(2,128)S(1)} %get-tuple-element.20), channel_id=1, source_target_pairs={{0,1},{1,0},{2,3},{3,2},{4,5},{5,4},{6,7},{7,6},{8,9},{9,8},{10,11... | collective-permute-start | bytes 27656 | tf_op jit(solution)/shard_map/ppermute | solution.py:241
